TPU v7x, 512 devices: a whole 4x4x16 slice. The times are simulated.
512 devices in a mesh: tm: 16 (over x, z_hi, core), tok: 32 (over z_lo, y).
Axes of the slice: x: 4, y: 4, z: 16 (z_hi: 2, z_lo: 8; z = z_hi * 8 + z_lo), core: 2. Of those that a mesh axis runs over, the one named last changes fastest.
Arguments:
- queries: bfloat16 [64, 768, 1152], P('tm', 'tok'), may hold values from -6 to 6
- keys: bfloat16 [64, 768, 1152], P('tm', 'tok'), may hold values from -6 to 6
- values: bfloat16 [64, 768, 1152], P('tm', 'tok'), may hold values from -6 to 6
- out_grad: bfloat16 [64, 768, 1152], P('tm', 'tok'), may hold values from -160 to 160
- time_bias: float32 [16, 16], replicated, may hold values from 2.5 to 5.5
Outputs:
- grad_queries: bfloat16 [64, 768, 1152], P('tm', 'tok')
- grad_keys: bfloat16 [64, 768, 1152], P('tm', 'tok')
- grad_values: bfloat16 [64, 768, 1152], P('tm', 'tok')
All inputs are finite; a program needn't handle non-finite values.
Results may differ from a plain program's by a relative error of at most 0.0091.
Values may be sent and summed in bfloat16 or wider, within the bound.
A program may use at most 128 MiB of HBM per device.

v0:
```python
import jax
import jax.numpy as jnp
from jax import lax
from jax.sharding import PartitionSpec as P


def passed_along(value, axis, steps):
    count = lax.axis_size(axis)
    first, last = (max(0, -steps), min(count, count - steps))
    return lax.ppermute(value, axis, [(source, source + steps) for source in range(first, last)])


def round_half(tensor):
    return lax.optimization_barrier(tensor.astype(jnp.bfloat16)).astype(jnp.float32)


def head_view(tensor, head_count):
    return tensor.reshape(
        tensor.shape[0], tensor.shape[1], head_count, tensor.shape[2] // head_count
    )


def block_rows(length):
    block_size = min(length, 640)
    while length % block_size:
        block_size -= 1
    return block_size


def near_frames(stacked, hop_count):
    pieces = []
    for distance in list(range(hop_count, 0, -1)) + list(range(-1, -hop_count - 1, -1)):
        pieces.append(passed_along(stacked, "tm", distance))
    return jnp.concatenate(pieces[:hop_count] + [stacked] + pieces[hop_count:], axis=1)


def head_sum(product, indicator):
    frames, tok_rows, model_width = product.shape
    summed = jnp.dot(
        product.reshape(frames * tok_rows, model_width),
        indicator,
        precision=lax.Precision.HIGHEST,
        preferred_element_type=jnp.float32,
    )
    return summed.reshape(frames, tok_rows, indicator.shape[1])


def spatial_item(packed, partial_value, score_scale, head_dim):
    length = packed.shape[1]
    block_size = block_rows(length)
    block_count = length // block_size
    query_all = packed[:head_dim]
    key_all = packed[head_dim : 2 * head_dim]
    value_all = packed[2 * head_dim : 3 * head_dim]
    grad_all = packed[3 * head_dim :]
    first_dims = (((0,), (0,)), ((), ()))
    row_dims = (((1,), (0,)), ((), ()))
    last_dims = (((1,), (1,)), ((), ()))

    def advance(carried, block_index):
        key_sum, value_sum = carried
        block_start = block_index * block_size
        query_block = lax.dynamic_slice_in_dim(query_all, block_start, block_size, 1)
        grad_block = lax.dynamic_slice_in_dim(grad_all, block_start, block_size, 1)
        part_block = lax.dynamic_slice_in_dim(partial_value, block_start, block_size, 1)
        scores = (
            lax.dot_general(query_block, key_all, first_dims, preferred_element_type=jnp.float32)
            * score_scale
        )
        dot_values = lax.dot_general(
            grad_block, value_all, first_dims, preferred_element_type=jnp.float32
        )
        joined_max = jnp.maximum(jnp.max(scores, axis=1), part_block[0])
        spread = jnp.exp(scores - joined_max[:, None])
        carried_scale = jnp.exp(part_block[0] - joined_max)
        total_mass = jnp.sum(spread, axis=1) + part_block[1] * carried_scale
        log_total = joined_max + jnp.log(total_mass)
        delta_value = (
            jnp.sum(spread * dot_values, axis=1) + part_block[2] * carried_scale
        ) / total_mass
        weights = jnp.exp(scores - log_total[:, None])
        rounded = lax.optimization_barrier(weights.astype(jnp.bfloat16))
        slopes = (rounded.astype(jnp.float32) * (dot_values - delta_value[:, None])).astype(
            jnp.bfloat16
        )
        grad_query = (
            lax.dot_general(key_all, slopes, last_dims, preferred_element_type=jnp.float32)
            * score_scale
        )
        key_sum = (
            key_sum
            + lax.dot_general(query_block, slopes, row_dims, preferred_element_type=jnp.float32)
            * score_scale
        )
        value_sum = value_sum + lax.dot_general(
            grad_block, rounded, row_dims, preferred_element_type=jnp.float32
        )
        return ((key_sum, value_sum), (grad_query, jnp.stack([log_total, delta_value])))

    zeros = jnp.zeros((head_dim, length), jnp.float32)
    (key_sum, value_sum), (grad_blocks, stat_blocks) = lax.scan(
        advance, (zeros, zeros), jnp.arange(block_count)
    )
    grad_query = grad_blocks.transpose(1, 0, 2).reshape(head_dim, length)
    stat_all = stat_blocks.transpose(1, 0, 2).reshape(2, length)
    return (jnp.concatenate([grad_query, key_sum, value_sum], axis=0), stat_all)


def body(queries, keys, values, out_grad, time_bias):
    frames, tok_rows, model_width = queries.shape
    head_count, offset_count = time_bias.shape
    band_reach = offset_count // 2
    head_dim = model_width // head_count
    groups = lax.axis_size("tok")
    hop_count = -(-band_reach // frames)
    score_scale = head_dim ** (-0.5)
    item_count = frames * head_count // groups
    total_frames = frames * lax.axis_size("tm")
    frame_ids = lax.axis_index("tm") * frames + jnp.arange(frames)
    offsets = [
        offset_step for offset_step in range(-band_reach, band_reach + 1) if offset_step != 0
    ]
    centre = hop_count * frames
    indicator = (
        jnp.arange(model_width)[:, None] // head_dim == jnp.arange(head_count)[None, :]
    ).astype(jnp.float32)
    query_wide = queries.astype(jnp.float32)
    grad_wide = out_grad.astype(jnp.float32)

    def widen(per_head):
        return jnp.repeat(per_head, head_dim, axis=-1)

    extended = near_frames(jnp.stack([keys, values]), hop_count)
    key_ext = extended[0]
    value_ext = extended[1]
    score_list = []
    dot_list = []
    for column, offset in enumerate(offsets):
        key_near = lax.slice_in_dim(
            key_ext, centre + offset, centre + offset + frames, axis=0
        ).astype(jnp.float32)
        value_near = lax.slice_in_dim(
            value_ext, centre + offset, centre + offset + frames, axis=0
        ).astype(jnp.float32)
        raw_score = head_sum(query_wide * key_near, indicator)
        inside = ((frame_ids + offset >= 0) & (frame_ids + offset < total_frames))[:, None, None]
        score_list.append(
            jnp.where(inside, raw_score * score_scale + time_bias[:, column], -jnp.inf)
        )
        dot_list.append(head_sum(grad_wide * value_near, indicator))
    score_time = jnp.stack(score_list)
    dot_time = jnp.stack(dot_list)
    peak_score = jnp.max(score_time, axis=0)
    spread = jnp.exp(score_time - peak_score)
    mass_total = jnp.sum(spread, axis=0)
    moment = jnp.sum(spread * dot_time, axis=0)
    partial_value = (
        jnp.stack([peak_score, mass_total, moment])
        .transpose(1, 3, 0, 2)
        .reshape(groups, item_count, 3, tok_rows)
    )
    bundle = jnp.stack(
        [
            head_view(queries, head_count),
            head_view(keys, head_count),
            head_view(values, head_count),
            head_view(out_grad, head_count),
        ]
    ).transpose(1, 3, 0, 4, 2)
    bundle = bundle.reshape(groups, item_count, 4 * head_dim, tok_rows)
    arrived = lax.all_to_all(bundle, "tok", split_axis=0, concat_axis=3, tiled=True)
    partial_in = lax.all_to_all(partial_value, "tok", split_axis=0, concat_axis=3, tiled=True)

    def one_item(item_pair):
        return spatial_item(item_pair[0], item_pair[1], score_scale, head_dim)

    grads_head, stats_head = lax.map(one_item, (arrived[0], partial_in[0]))
    returned, totals = (
        lax.all_to_all(grads_head, "tok", split_axis=2, concat_axis=0, tiled=True),
        lax.all_to_all(stats_head, "tok", split_axis=2, concat_axis=0, tiled=True),
    )
    returned = (
        returned.reshape(frames, head_count, 3, head_dim, tok_rows)
        .transpose(2, 0, 4, 1, 3)
        .reshape(3, frames, tok_rows, model_width)
    )
    totals = totals.reshape(frames, head_count, 2, tok_rows).transpose(2, 0, 3, 1)
    log_total = totals[0]
    delta_value = totals[1]
    grad_query = returned[0]
    grad_key = returned[1]
    grad_value = returned[2]
    ext_frames = key_ext.shape[0]
    key_parts = [None] * ext_frames
    value_parts = [None] * ext_frames
    for column, offset in enumerate(offsets):
        rounded = round_half(jnp.exp(score_time[column] - log_total))
        slope_value = round_half(rounded * (dot_time[column] - delta_value))
        slope_wide = widen(slope_value)
        key_near = lax.slice_in_dim(
            key_ext, centre + offset, centre + offset + frames, axis=0
        ).astype(jnp.float32)
        grad_query = grad_query + score_scale * slope_wide * key_near
        rounded_wide = widen(rounded)
        for frame in range(frames):
            target = centre + offset + frame
            key_term = score_scale * slope_wide[frame] * query_wide[frame]
            value_term = rounded_wide[frame] * grad_wide[frame]
            key_parts[target] = (
                key_term if key_parts[target] is None else key_parts[target] + key_term
            )
            value_parts[target] = (
                value_term if value_parts[target] is None else value_parts[target] + value_term
            )
    blank = jnp.zeros((tok_rows, model_width), jnp.float32)
    key_list = [blank if piece is None else piece for piece in key_parts]
    value_list = [blank if piece is None else piece for piece in value_parts]
    outbound = jnp.stack([jnp.stack(key_list), jnp.stack(value_list)])
    home_sum = lax.slice_in_dim(outbound, centre, centre + frames, axis=1)
    move_list = [
        ((hop_count - distance) * frames, -distance) for distance in range(1, hop_count + 1)
    ]
    move_list = move_list + [
        ((hop_count + distance) * frames, distance) for distance in range(1, hop_count + 1)
    ]
    for block_start, shift_by in move_list:
        piece_block = lax.slice_in_dim(outbound, block_start, block_start + frames, axis=1)
        home_sum = home_sum + passed_along(piece_block, "tm", shift_by)
    grad_key = grad_key + home_sum[0]
    grad_value = grad_value + home_sum[1]
    return (
        grad_query.astype(jnp.bfloat16),
        grad_key.astype(jnp.bfloat16),
        grad_value.astype(jnp.bfloat16),
    )


def solution(mesh):
    in_specs = (
        P("tm", "tok", None),
        P("tm", "tok", None),
        P("tm", "tok", None),
        P("tm", "tok", None),
        P(),
    )
    out_specs = (P("tm", "tok", None), P("tm", "tok", None), P("tm", "tok", None))
    return jax.shard_map(body, mesh=mesh, in_specs=in_specs, out_specs=out_specs, check_vma=False)
```

profile of v0, /device:TPU:35, one launch (start us, length us, event | category | flops | bytes accessed | tf_op | source)
XLA Modules:
  0.0 809.1 jit_solution(9122779407584867671)
XLA Ops:
  2.5 15.1 %collective-permute-start.1 = (bf16[2,4,24,1152]{3,2,1,0:T(8,128)(2,1)}, bf16[2,4,24,1152]{3,2,1,0:T(8,128)(2,1)S(1)}, u32[]{:S(2)}, u32[]{:S(2)}) collective-permute-start(bf16[2,4,24,1152]{3,2,1,0:T(8,128)(2,1)} %pad_maximum_fusion.2), channel_id=1, source_target_pairs={{0,32},{32,64},{64,96},{96,128},{128,160},{160,192},{192,224},{224... | collective-permute-start | bytes 1327112 | tf_op jit(solution)/shard_map/ppermute | solution.py:10
  19.6 2.0 collective-permute-start
  21.6 12.9 %collective-permute-start.3 = (bf16[2,4,24,1152]{3,2,1,0:T(8,128)(2,1)}, bf16[2,4,24,1152]{3,2,1,0:T(8,128)(2,1)}, u32[]{:S(2)}, u32[]{:S(2)}) collective-permute-start(bf16[2,4,24,1152]{3,2,1,0:T(8,128)(2,1)} %pad_maximum_fusion.2), channel_id=1, source_target_pairs={{64,0},{96,32},{128,64},{160,96},{192,128},{224,160},{256,192},{28... | collective-permute-start | bytes 1327112 | tf_op jit(solution)/shard_map/ppermute | solution.py:10
  52.4 30.8 %collective-permute-done = bf16[2,4,24,1152]{3,2,1,0:T(8,128)(2,1)S(1)} collective-permute-done((bf16[2,4,24,1152]{3,2,1,0:T(8,128)(2,1)}, bf16[2,4,24,1152]{3,2,1,0:T(8,128)(2,1)S(1)}, u32[]{:S(2)}, u32[]{:S(2)}) %collective-permute-start) | collective-permute-done | bytes 442400 | tf_op jit(solution)/shard_map/ppermute | solution.py:10
  84.4 30.2 %collective-permute-done.3 = bf16[2,4,24,1152]{3,2,1,0:T(8,128)(2,1)} collective-permute-done((bf16[2,4,24,1152]{3,2,1,0:T(8,128)(2,1)}, bf16[2,4,24,1152]{3,2,1,0:T(8,128)(2,1)}, u32[]{:S(2)}, u32[]{:S(2)}) %collective-permute-start.3) | collective-permute-done | bytes 442400 | tf_op jit(solution)/shard_map/ppermute | solution.py:10
  115.7 4.1 convert_multiply_fusion.1
  122.2 2.0 fusion.79
  125.5 2.0 fusion.80
  128.9 2.0 fusion.81
  132.2 2.0 fusion.82
  138.9 2.0 fusion.84
  142.3 2.0 fusion.85
  145.6 2.0 fusion.86
  149.0 2.0 fusion.87
  152.3 2.0 fusion.88
  155.7 2.0 fusion.89
  159.0 2.0 fusion.90
  162.4 2.0 fusion.91
  165.7 2.0 fusion.92
  169.1 2.0 fusion.93
  211.8 26.1 %all-to-all-start.1 = ((f32[32,1,144]{2,1,0:T(1,128)}), f32[32,1,144]{2,1,0:T(1,128)S(1)}, u32[]{:S(2)}, u32[]{:S(2)}) async-start(f32[32,1,144]{2,1,0:T(1,128)} %reshape.2367), calls=%async_computation.1 | async-start | bytes 65536 | tf_op jit(solution)/shard_map/all_to_all | solution.py:172
  237.9 5.7 maximum_bitcast_fusion.2
  245.5 2.8 all-to-all-done.1
  248.3 9.2 %all-to-all-start = ((bf16[32,2,288,24]{2,3,1,0:T(8,128)(2,1)}), bf16[32,2,288,24]{2,3,1,0:T(8,128)(2,1)S(1)}, u32[]{:S(2)}, u32[]{:S(2)}) async-start(bf16[32,2,288,24]{2,3,1,0:T(8,128)(2,1)} %reshape.2294), calls=%async_computation | async-start | bytes 2359296 | tf_op jit(solution)/shard_map/all_to_all | solution.py:171
  259.1 49.9 %all-to-all-done = bf16[32,2,288,24]{2,3,1,0:T(8,128)(2,1)S(1)} async-done(((bf16[32,2,288,24]{2,3,1,0:T(8,128)(2,1)}), bf16[32,2,288,24]{2,3,1,0:T(8,128)(2,1)S(1)}, u32[]{:S(2)}, u32[]{:S(2)}) %all-to-all-start) | async-done | bytes 884768 | tf_op jit(solution)/shard_map/all_to_all | solution.py:171
  311.7 17.4 %while.30 = (s32[]{:T(128)}, f32[2,216,768]{2,1,0:T(8,128)}, f32[2,2,768]{2,1,0:T(2,128)S(1)}, bf16[2,288,768]{2,1,0:T(8,128)(2,1)S(1)}, f32[2,3,768]{2,1,0:T(4,...) while((s32[]{:T(128)}, f32[2,216,768]{2,1,0:T(8,128)}, ...), condition=%wide.region_8.9_spmd, body=%wide.region_2.8_spmd.sunk | while | flops 216517248 | bytes 13725843 | solution.py:177
  311.8 7.6 while.31
  320.5 7.6 while.31
  330.5 11.2 %all-to-all-start.3 = ((f32[2,2,768]{1,0,2:T(2,128)}), f32[2,2,768]{1,0,2:T(2,128)S(1)}, u32[]{:S(2)}, u32[]{:S(2)}) async-start(f32[2,2,768]{1,0,2:T(2,128)} %copy.564), calls=%async_computation.3 | async-start | bytes 1572864 | tf_op jit(solution)/shard_map/all_to_all | solution.py:180
  351.2 2.1 copy.560
  353.4 25.5 %all-to-all-done.3 = f32[2,2,768]{1,0,2:T(2,128)S(1)} async-done(((f32[2,2,768]{1,0,2:T(2,128)}), f32[2,2,768]{1,0,2:T(2,128)S(1)}, u32[]{:S(2)}, u32[]{:S(2)}) %all-to-all-start.3) | async-done | bytes 12320 | tf_op jit(solution)/shard_map/all_to_all | solution.py:180
  378.9 9.5 %all-to-all-start.2 = ((f32[2,216,768]{1,0,2:T(2,128)}), f32[2,216,768]{1,0,2:T(2,128)}, u32[]{:S(2)}, u32[]{:S(2)}) async-start(f32[2,216,768]{1,0,2:T(2,128)} %copy.560), calls=%async_computation.2 | async-start | bytes 3145728 | tf_op jit(solution)/shard_map/all_to_all | solution.py:179
  535.6 3.2 fusion.54
  538.8 3.5 collective-permute-start.4
  542.4 7.7 collective-permute-start.5
  550.0 11.1 %collective-permute-start.6 = (f32[2,4,24,1152]{3,2,1,0:T(8,128)}, f32[2,4,24,1152]{3,2,1,0:T(8,128)}, u32[]{:S(2)}, u32[]{:S(2)}) collective-permute-start(f32[2,4,24,1152]{3,2,1,0:T(8,128)} %get-tuple-element.213), channel_id=1, source_target_pairs={{0,32},{32,64},{64,96},{96,128},{128,160},{160,192},{192,224},{224... | collective-permute-start | bytes 2654216 | tf_op jit(solution)/shard_map/ppermute | solution.py:10
  561.2 7.2 collective-permute-start.7
  592.2 3.0 collective-permute-done.4
  595.2 9.9 %collective-permute-done.5 = f32[2,4,24,1152]{3,2,1,0:T(8,128)} collective-permute-done((f32[2,4,24,1152]{3,2,1,0:T(8,128)}, f32[2,4,24,1152]{3,2,1,0:T(8,128)}, u32[]{:S(2)}, u32[]{:S(2)}) %collective-permute-start.5) | collective-permute-done | bytes 884768 | tf_op jit(solution)/shard_map/ppermute | solution.py:10
  605.1 36.9 %collective-permute-done.6 = f32[2,4,24,1152]{3,2,1,0:T(8,128)} collective-permute-done((f32[2,4,24,1152]{3,2,1,0:T(8,128)}, f32[2,4,24,1152]{3,2,1,0:T(8,128)}, u32[]{:S(2)}, u32[]{:S(2)}) %collective-permute-start.6) | collective-permute-done | bytes 884768 | tf_op jit(solution)/shard_map/ppermute | solution.py:10
  642.0 140.7 %collective-permute-done.7 = f32[2,4,24,1152]{3,2,1,0:T(8,128)} collective-permute-done((f32[2,4,24,1152]{3,2,1,0:T(8,128)}, f32[2,4,24,1152]{3,2,1,0:T(8,128)}, u32[]{:S(2)}, u32[]{:S(2)}) %collective-permute-start.7) | collective-permute-done | bytes 884768 | tf_op jit(solution)/shard_map/ppermute | solution.py:10
  782.7 3.2 fusion.53
  788.9 3.4 reshape.2312
  792.2 2.5 fusion.243
  797.3 2.3 copy.563
  799.7 2.2 squeeze.38
  801.9 2.1 fusion.74
  804.1 4.5 fusion.77
  (1255 shorter events, 292.5 us)
Async XLA Ops:
  0.6 42.2 %copy-start.25 = (bf16[4,24,1152]{2,1,0:T(8,128)(2,1)S(1)}, bf16[4,24,1152]{2,1,0:T(8,128)(2,1)}, u32[]{:S(2)}) copy-start(bf16[4,24,1152]{2,1,0:T(8,128)(2,1)} %param.9) | copy-start | bytes 663556
  2.5 81.5 %collective-permute-start.1 = (bf16[2,4,24,1152]{3,2,1,0:T(8,128)(2,1)}, bf16[2,4,24,1152]{3,2,1,0:T(8,128)(2,1)S(1)}, u32[]{:S(2)}, u32[]{:S(2)}) collective-permute-start(bf16[2,4,24,1152]{3,2,1,0:T(8,128)(2,1)} %pad_maximum_fusion.2), channel_id=1, source_target_pairs={{0,32},{32,64},{64,96},{96,128},{128,160},{160,192},{192,224},{224... | collective-permute-start | bytes 1327112 | tf_op jit(solution)/shard_map/ppermute | solution.py:10
  17.6 66.4 %collective-permute-start.2 = (bf16[2,4,24,1152]{3,2,1,0:T(8,128)(2,1)}, bf16[2,4,24,1152]{3,2,1,0:T(8,128)(2,1)S(1)}, u32[]{:S(2)}, u32[]{:S(2)}) collective-permute-start(bf16[2,4,24,1152]{3,2,1,0:T(8,128)(2,1)} %pad_maximum_fusion.2), channel_id=1, source_target_pairs={{32,0},{64,32},{96,64},{128,96},{160,128},{192,160},{224,192},{256... | collective-permute-start | bytes 1327112 | tf_op jit(solution)/shard_map/ppermute | solution.py:10
  19.6 63.7 %collective-permute-start = (bf16[2,4,24,1152]{3,2,1,0:T(8,128)(2,1)}, bf16[2,4,24,1152]{3,2,1,0:T(8,128)(2,1)S(1)}, u32[]{:S(2)}, u32[]{:S(2)}) collective-permute-start(bf16[2,4,24,1152]{3,2,1,0:T(8,128)(2,1)} %pad_maximum_fusion.2), channel_id=1, source_target_pairs={{0,64},{32,96},{64,128},{96,160},{128,192},{160,224},{192,256},{22... | collective-permute-start | bytes 1327112 | tf_op jit(solution)/shard_map/ppermute | solution.py:10
  21.6 93.0 %collective-permute-start.3 = (bf16[2,4,24,1152]{3,2,1,0:T(8,128)(2,1)}, bf16[2,4,24,1152]{3,2,1,0:T(8,128)(2,1)}, u32[]{:S(2)}, u32[]{:S(2)}) collective-permute-start(bf16[2,4,24,1152]{3,2,1,0:T(8,128)(2,1)} %pad_maximum_fusion.2), channel_id=1, source_target_pairs={{64,0},{96,32},{128,64},{160,96},{192,128},{224,160},{256,192},{28... | collective-permute-start | bytes 1327112 | tf_op jit(solution)/shard_map/ppermute | solution.py:10
  48.8 35.3 %copy-start.19 = (bf16[4,24,1152]{2,1,0:T(8,128)(2,1)S(1)}, bf16[4,24,1152]{2,1,0:T(8,128)(2,1)}, u32[]{:S(2)}) copy-start(bf16[4,24,1152]{2,1,0:T(8,128)(2,1)} %param.11) | copy-start | bytes 663556
  48.8 35.3 %copy-start.20 = (bf16[4,24,1152]{2,1,0:T(8,128)(2,1)S(1)}, bf16[4,24,1152]{2,1,0:T(8,128)(2,1)}, u32[]{:S(2)}) copy-start(bf16[4,24,1152]{2,1,0:T(8,128)(2,1)} %param.10) | copy-start | bytes 663556
  84.0 121.8 %copy-start.6 = (bf16[2,4,24,1152]{3,2,1,0:T(8,128)(2,1)}, bf16[2,4,24,1152]{3,2,1,0:T(8,128)(2,1)S(1)}, u32[]{:S(2)}) copy-start(bf16[2,4,24,1152]{3,2,1,0:T(8,128)(2,1)S(1)} %collective-permute-done.2) | copy-start | bytes 1327108
  84.1 116.3 %copy-start.4 = (bf16[2,4,24,1152]{3,2,1,0:T(8,128)(2,1)}, bf16[2,4,24,1152]{3,2,1,0:T(8,128)(2,1)S(1)}, u32[]{:S(2)}) copy-start(bf16[2,4,24,1152]{3,2,1,0:T(8,128)(2,1)S(1)} %collective-permute-done.1) | copy-start | bytes 1327108
  84.2 35.6 %copy-start.11 = (bf16[2,8,24,1152]{3,2,1,0:T(8,128)(2,1)}, bf16[2,8,24,1152]{3,2,1,0:T(8,128)(2,1)S(1)}, u32[]{:S(2)}) copy-start(bf16[2,8,24,1152]{3,2,1,0:T(8,128)(2,1)S(1)} %constant_dynamic-update-slice_fusion.1) | copy-start | bytes 2654212
  84.4 118.3 %copy-start.2 = (bf16[2,8,24,1152]{3,2,1,0:T(8,128)(2,1)}, bf16[2,8,24,1152]{3,2,1,0:T(8,128)(2,1)S(1)}, u32[]{:S(2)}) copy-start(bf16[2,8,24,1152]{3,2,1,0:T(8,128)(2,1)S(1)} %get-tuple-element.232) | copy-start | bytes 2654212
  84.4 120.6 %copy-start = (bf16[2,8,24,1152]{3,2,1,0:T(8,128)(2,1)}, bf16[2,8,24,1152]{3,2,1,0:T(8,128)(2,1)S(1)}, u32[]{:S(2)}) copy-start(bf16[2,8,24,1152]{3,2,1,0:T(8,128)(2,1)S(1)} %get-tuple-element.231) | copy-start | bytes 2654212
  115.7 92.5 %copy-start.9 = (bf16[2,8,24,1152]{3,2,1,0:T(8,128)(2,1)}, bf16[2,8,24,1152]{3,2,1,0:T(8,128)(2,1)S(1)}, u32[]{:S(2)}) copy-start(bf16[2,8,24,1152]{3,2,1,0:T(8,128)(2,1)S(1)} %constant_dynamic-update-slice_fusion.3) | copy-start | bytes 2654212
  211.8 36.6 %all-to-all-start.1 = ((f32[32,1,144]{2,1,0:T(1,128)}), f32[32,1,144]{2,1,0:T(1,128)S(1)}, u32[]{:S(2)}, u32[]{:S(2)}) async-start(f32[32,1,144]{2,1,0:T(1,128)} %reshape.2367), calls=%async_computation.1 | async-start | bytes 65536 | tf_op jit(solution)/shard_map/all_to_all | solution.py:172
  248.3 60.7 %all-to-all-start = ((bf16[32,2,288,24]{2,3,1,0:T(8,128)(2,1)}), bf16[32,2,288,24]{2,3,1,0:T(8,128)(2,1)S(1)}, u32[]{:S(2)}, u32[]{:S(2)}) async-start(bf16[32,2,288,24]{2,3,1,0:T(8,128)(2,1)} %reshape.2294), calls=%async_computation | async-start | bytes 2359296 | tf_op jit(solution)/shard_map/all_to_all | solution.py:171
  330.5 48.4 %all-to-all-start.3 = ((f32[2,2,768]{1,0,2:T(2,128)}), f32[2,2,768]{1,0,2:T(2,128)S(1)}, u32[]{:S(2)}, u32[]{:S(2)}) async-start(f32[2,2,768]{1,0,2:T(2,128)} %copy.564), calls=%async_computation.3 | async-start | bytes 1572864 | tf_op jit(solution)/shard_map/all_to_all | solution.py:180
  353.3 36.3 %copy-start.182 = (f32[4,24,16]{1,2,0:T(8,128)S(1)}, f32[4,24,16]{1,2,0:T(8,128)}, u32[]{:S(2)}) copy-start(f32[4,24,16]{1,2,0:T(8,128)} %copy-done.181) | copy-start | bytes 18436
  353.3 36.3 %copy-start.184 = (f32[4,24,16]{1,2,0:T(8,128)S(1)}, f32[4,24,16]{1,2,0:T(8,128)}, u32[]{:S(2)}) copy-start(f32[4,24,16]{1,2,0:T(8,128)} %copy-done.183) | copy-start | bytes 18436
  353.3 36.3 %copy-start.186 = (f32[4,24,16]{1,2,0:T(8,128)S(1)}, f32[4,24,16]{1,2,0:T(8,128)}, u32[]{:S(2)}) copy-start(f32[4,24,16]{1,2,0:T(8,128)} %copy-done.185) | copy-start | bytes 18436
  353.3 36.3 %copy-start.188 = (f32[4,24,16]{1,2,0:T(8,128)S(1)}, f32[4,24,16]{1,2,0:T(8,128)}, u32[]{:S(2)}) copy-start(f32[4,24,16]{1,2,0:T(8,128)} %copy-done.187) | copy-start | bytes 18436
  353.3 36.3 %copy-start.190 = (f32[4,24,16]{1,2,0:T(8,128)S(1)}, f32[4,24,16]{1,2,0:T(8,128)}, u32[]{:S(2)}) copy-start(f32[4,24,16]{1,2,0:T(8,128)} %copy-done.189) | copy-start | bytes 18436
  353.3 36.3 %copy-start.192 = (f32[4,24,16]{1,2,0:T(8,128)S(1)}, f32[4,24,16]{1,2,0:T(8,128)}, u32[]{:S(2)}) copy-start(f32[4,24,16]{1,2,0:T(8,128)} %copy-done.191) | copy-start | bytes 18436
  353.3 36.3 %copy-start.194 = (f32[4,24,16]{1,2,0:T(8,128)S(1)}, f32[4,24,16]{1,2,0:T(8,128)}, u32[]{:S(2)}) copy-start(f32[4,24,16]{1,2,0:T(8,128)} %copy-done.193) | copy-start | bytes 18436
  353.3 36.3 %copy-start.196 = (f32[4,24,16]{1,2,0:T(8,128)S(1)}, f32[4,24,16]{1,2,0:T(8,128)}, u32[]{:S(2)}) copy-start(f32[4,24,16]{1,2,0:T(8,128)} %copy-done.195) | copy-start | bytes 18436
  353.3 36.3 %copy-start.198 = (f32[4,24,16]{1,2,0:T(8,128)S(1)}, f32[4,24,16]{1,2,0:T(8,128)}, u32[]{:S(2)}) copy-start(f32[4,24,16]{1,2,0:T(8,128)} %copy-done.197) | copy-start | bytes 18436
  353.3 36.4 %copy-start.167 = (f32[4,24,16]{1,2,0:T(8,128)S(1)}, f32[4,24,16]{1,2,0:T(8,128)}, u32[]{:S(2)}) copy-start(f32[4,24,16]{1,2,0:T(8,128)} %copy-done.166) | copy-start | bytes 18436
  353.3 36.4 %copy-start.169 = (f32[4,24,16]{1,2,0:T(8,128)S(1)}, f32[4,24,16]{1,2,0:T(8,128)}, u32[]{:S(2)}) copy-start(f32[4,24,16]{1,2,0:T(8,128)} %copy-done.168) | copy-start | bytes 18436
  353.3 36.5 %copy-start.178 = (f32[4,24,16]{1,2,0:T(8,128)S(1)}, f32[4,24,16]{1,2,0:T(8,128)}, u32[]{:S(2)}) copy-start(f32[4,24,16]{1,2,0:T(8,128)} %copy-done.177) | copy-start | bytes 18436
  353.3 36.5 %copy-start.180 = (f32[4,24,16]{1,2,0:T(8,128)S(1)}, f32[4,24,16]{1,2,0:T(8,128)}, u32[]{:S(2)}) copy-start(f32[4,24,16]{1,2,0:T(8,128)} %copy-done.179) | copy-start | bytes 18436
  353.4 36.5 %copy-start.204 = (f32[4,24,16]{1,0,2:T(4,128)S(1)}, f32[4,24,16]{1,0,2:T(4,128)}, u32[]{:S(2)}) copy-start(f32[4,24,16]{1,0,2:T(4,128)} %squeeze_stack_reshape.54) | copy-start | bytes 18436
  353.4 36.5 %copy-start.205 = (f32[4,24,16]{1,0,2:T(4,128)S(1)}, f32[4,24,16]{1,0,2:T(4,128)}, u32[]{:S(2)}) copy-start(f32[4,24,16]{1,0,2:T(4,128)} %squeeze_stack_reshape.55) | copy-start | bytes 18436
  353.4 36.5 %copy-start.206 = (f32[4,24,16]{1,0,2:T(4,128)S(1)}, f32[4,24,16]{1,0,2:T(4,128)}, u32[]{:S(2)}) copy-start(f32[4,24,16]{1,0,2:T(4,128)} %squeeze_stack_reshape.56) | copy-start | bytes 18436
  353.4 36.5 %copy-start.207 = (f32[4,24,16]{1,0,2:T(4,128)S(1)}, f32[4,24,16]{1,0,2:T(4,128)}, u32[]{:S(2)}) copy-start(f32[4,24,16]{1,0,2:T(4,128)} %squeeze_stack_reshape.57) | copy-start | bytes 18436
  353.4 36.5 %copy-start.208 = (f32[4,24,16]{1,0,2:T(4,128)S(1)}, f32[4,24,16]{1,0,2:T(4,128)}, u32[]{:S(2)}) copy-start(f32[4,24,16]{1,0,2:T(4,128)} %squeeze_stack_reshape.58) | copy-start | bytes 18436
  378.9 407.0 %all-to-all-start.2 = ((f32[2,216,768]{1,0,2:T(2,128)}), f32[2,216,768]{1,0,2:T(2,128)}, u32[]{:S(2)}, u32[]{:S(2)}) async-start(f32[2,216,768]{1,0,2:T(2,128)} %copy.560), calls=%async_computation.2 | async-start | bytes 3145728 | tf_op jit(solution)/shard_map/all_to_all | solution.py:179
  390.0 80.4 %copy-start.142 = (bf16[4,24,16]{1,2,0:T(8,128)(2,1)}, bf16[4,24,16]{1,2,0:T(8,128)(2,1)S(1)}, u32[]{:S(2)}) copy-start(bf16[4,24,16]{1,2,0:T(8,128)(2,1)S(1)} %get-tuple-element.253) | copy-start | bytes 9220
  390.0 84.3 %copy-start.140 = (bf16[4,24,16]{1,2,0:T(8,128)(2,1)}, bf16[4,24,16]{1,2,0:T(8,128)(2,1)S(1)}, u32[]{:S(2)}) copy-start(bf16[4,24,16]{1,2,0:T(8,128)(2,1)S(1)} %get-tuple-element.254) | copy-start | bytes 9220
  390.0 90.1 %copy-start.138 = (bf16[4,24,16]{1,2,0:T(8,128)(2,1)}, bf16[4,24,16]{1,2,0:T(8,128)(2,1)S(1)}, u32[]{:S(2)}) copy-start(bf16[4,24,16]{1,2,0:T(8,128)(2,1)S(1)} %get-tuple-element.255) | copy-start | bytes 9220
  390.0 93.0 %copy-start.136 = (bf16[4,24,16]{1,2,0:T(8,128)(2,1)}, bf16[4,24,16]{1,2,0:T(8,128)(2,1)S(1)}, u32[]{:S(2)}) copy-start(bf16[4,24,16]{1,2,0:T(8,128)(2,1)S(1)} %get-tuple-element.256) | copy-start | bytes 9220
  393.2 96.7 %copy-start.152 = (bf16[4,24,16]{1,2,0:T(8,128)(2,1)}, bf16[4,24,16]{1,2,0:T(8,128)(2,1)S(1)}, u32[]{:S(2)}) copy-start(bf16[4,24,16]{1,2,0:T(8,128)(2,1)S(1)} %get-tuple-element.260) | copy-start | bytes 9220
  393.2 100.5 %copy-start.150 = (bf16[4,24,16]{1,2,0:T(8,128)(2,1)}, bf16[4,24,16]{1,2,0:T(8,128)(2,1)S(1)}, u32[]{:S(2)}) copy-start(bf16[4,24,16]{1,2,0:T(8,128)(2,1)S(1)} %get-tuple-element.261) | copy-start | bytes 9220
  393.2 104.4 %copy-start.148 = (bf16[4,24,16]{1,2,0:T(8,128)(2,1)}, bf16[4,24,16]{1,2,0:T(8,128)(2,1)S(1)}, u32[]{:S(2)}) copy-start(bf16[4,24,16]{1,2,0:T(8,128)(2,1)S(1)} %get-tuple-element.262) | copy-start | bytes 9220
  393.2 108.3 %copy-start.146 = (bf16[4,24,16]{1,2,0:T(8,128)(2,1)}, bf16[4,24,16]{1,2,0:T(8,128)(2,1)S(1)}, u32[]{:S(2)}) copy-start(bf16[4,24,16]{1,2,0:T(8,128)(2,1)S(1)} %get-tuple-element.263) | copy-start | bytes 9220
  393.2 112.1 %copy-start.144 = (bf16[4,24,16]{1,2,0:T(8,128)(2,1)}, bf16[4,24,16]{1,2,0:T(8,128)(2,1)S(1)}, u32[]{:S(2)}) copy-start(bf16[4,24,16]{1,2,0:T(8,128)(2,1)S(1)} %get-tuple-element.264) | copy-start | bytes 9220
  538.8 56.4 %collective-permute-start.4 = (f32[2,4,24,1152]{3,2,1,0:T(8,128)}, f32[2,4,24,1152]{3,2,1,0:T(8,128)}, u32[]{:S(2)}, u32[]{:S(2)}) collective-permute-start(f32[2,4,24,1152]{3,2,1,0:T(8,128)} %get-tuple-element.210), channel_id=1, source_target_pairs={{32,0},{64,32},{96,64},{128,96},{160,128},{192,160},{224,192},{256... | collective-permute-start | bytes 2654216 | tf_op jit(solution)/shard_map/ppermute | solution.py:10
  542.4 62.8 %collective-permute-start.5 = (f32[2,4,24,1152]{3,2,1,0:T(8,128)}, f32[2,4,24,1152]{3,2,1,0:T(8,128)}, u32[]{:S(2)}, u32[]{:S(2)}) collective-permute-start(f32[2,4,24,1152]{3,2,1,0:T(8,128)} %get-tuple-element.211), channel_id=1, source_target_pairs={{64,0},{96,32},{128,64},{160,96},{192,128},{224,160},{256,192},{28... | collective-permute-start | bytes 2654216 | tf_op jit(solution)/shard_map/ppermute | solution.py:10
  550.0 92.0 %collective-permute-start.6 = (f32[2,4,24,1152]{3,2,1,0:T(8,128)}, f32[2,4,24,1152]{3,2,1,0:T(8,128)}, u32[]{:S(2)}, u32[]{:S(2)}) collective-permute-start(f32[2,4,24,1152]{3,2,1,0:T(8,128)} %get-tuple-element.213), channel_id=1, source_target_pairs={{0,32},{32,64},{64,96},{96,128},{128,160},{160,192},{192,224},{224... | collective-permute-start | bytes 2654216 | tf_op jit(solution)/shard_map/ppermute | solution.py:10
  561.2 221.6 %collective-permute-start.7 = (f32[2,4,24,1152]{3,2,1,0:T(8,128)}, f32[2,4,24,1152]{3,2,1,0:T(8,128)}, u32[]{:S(2)}, u32[]{:S(2)}) collective-permute-start(f32[2,4,24,1152]{3,2,1,0:T(8,128)} %get-tuple-element.212), channel_id=1, source_target_pairs={{0,64},{32,96},{64,128},{96,160},{128,192},{160,224},{192,256},{22... | collective-permute-start | bytes 2654216 | tf_op jit(solution)/shard_map/ppermute | solution.py:10
  (215 other events, 1527.3 us)
where the time goes:
time: 822 us; the launch traced here: 809 us
  waiting for transfers between devices  330 us (40%)
  local copies, waits for them, and re-layouts  242 us (29%)
  starting transfers between devices  118 us (14%)
  other arithmetic  57.3 us (7%)
  matrix products  53.7 us (7%)
    ppermute x8, waiting for transfers between devices, passed_along(): lax.ppermute(value, axis, [(source, source + steps) for source in range(f...  251 us
    broadcast_in_dim x208, local copies, waits for them, and re-layouts, widen(): return jnp.repeat(per_head, head_dim, axis=-1)  64.8 us
    ppermute x8, starting transfers between devices, passed_along(): lax.ppermute(value, axis, [(source, source + steps) for source in range(f...  61.5 us
    mul x128, local copies, waits for them, and re-layouts, body(): key_term = score_scale * slope_wide[frame] * query_wide[frame]  54.1 us
    all_to_all x1, waiting for transfers between devices, body(): lax.all_to_all(bundle, 'tok', split_axis=0, concat_axis=3, tiled=True)  49.9 us
    dot_general x32, matrix products, head_sum(): jnp.dot(product.reshape(frames * tok_rows, model_width), indicator, preci...  46.6 us
    all_to_all x1, starting transfers between devices, body(): lax.all_to_all(partial_value, 'tok', split_axis=0, concat_axis=3, tiled=T...  26.1 us
    unnamed x521, local copies, waits for them, and re-layouts  25.9 us
  transfers between devices with their start and end apart: 12, of which 9 were waited for; matrix products, arithmetic and copies ran while one was open for 26% of the time, Pallas kernels for 0%

commit v1 on v0

v1 whole, which is shorter than its diff:
```python
import functools

import jax
import jax.numpy as jnp
from jax import lax
from jax.experimental import pallas as pl
from jax.experimental.pallas import tpu as pltpu
from jax.sharding import PartitionSpec as P

F32 = jnp.float32
BF16 = jnp.bfloat16
HEADS = 16
DIM = 72
TOKENS = 24
FRAMES = 4
WIDTH = HEADS * DIM
BAND = 8
GROUPS = 32
ROWS = GROUPS * TOKENS
PAIR = 2 * TOKENS
FWD = 112
BWD = 96
SCALE = DIM**-0.5
NT = (((1,), (1,)), ((), ()))


def device(x, z, core, y):
    return (x * 4 + lax.div(z, 8) * 2 + core, lax.rem(z, 8) * 4 + y)


def lanes_of(rows):
    return lax.broadcasted_iota(jnp.int32, (rows, 128), 1)


def pieces(source, target, width):
    found = []
    while width:
        step = min(width, 128 - source % 128, 128 - target % 128)
        low = target % 128
        found.append((source // 128, (target - source) % 128, low, low + step))
        source, target, width = source + step, target + step, width - step
    return found


def moved(value, shift):
    return value if shift == 0 else pltpu.roll(value, shift, 1)


def assemble(lane, parts):
    result = None
    for value, shift, low, high in reversed(parts):
        piece = moved(value, shift)
        result = piece if result is None else jnp.where(lane < high, piece, result)
    return result


def pack_heads(refs, send):
    def one_pair(pair, _):
        lane = lanes_of(PAIR)
        lane16 = lanes_of(16)
        tiles = []
        for ref in refs:
            wide = [ref[2 * pair + j].astype(F32) for j in range(2)]
            tiles.append(
                [
                    jnp.concatenate([w[:, 128 * t : 128 * t + 128] for w in wide], axis=0)
                    for t in range(WIDTH // 128)
                ]
            )
        for head in range(HEADS):
            start = head * DIM

            def run(array, first, target, width):
                return [
                    (tiles[array][t], s, a, b)
                    for t, s, a, b in pieces(start + first, target, width)
                ]

            upper = assemble(lane, run(0, 0, 0, 72) + run(1, 0, 72, 56))
            lower = assemble(lane, run(1, 56, 0, 16) + run(2, 0, 16, 72) + run(3, 0, 88, 40))
            rest = []
            for r in range(3):
                for value, s, a, b in run(3, 40, 32 * r, 32):
                    rest.append((value[16 * r : 16 * r + 16], s, a, b))
            rest = assemble(lane16, rest)
            send[head, pair, 0:48, :] = upper.astype(BF16)
            send[head, pair, 48:96, :] = lower.astype(BF16)
            send[head, pair, 96:112, :] = rest.astype(BF16)
        return 0

    lax.fori_loop(0, 2, one_pair, 0)


def unpack_blocks(block, q_ref, k_ref, v_ref, g_ref):
    def one(i, _):
        lane = lanes_of(PAIR)
        upper = block(i, 0, 48).astype(F32)
        lower = block(i, 48, 48).astype(F32)
        rest = block(i, 96, 16).astype(F32)
        q = jnp.where(lane < DIM, upper, 0.0)
        k = pltpu.roll(jnp.where(lane >= DIM, upper, lower), 56, 1)
        v = pltpu.roll(lower, 112, 1)
        tail = jnp.concatenate([pltpu.roll(rest, 40 - 32 * r + (128 if r == 2 else 0), 1) for r in range(3)], axis=0)
        g = jnp.where(lane < 40, pltpu.roll(lower, 40, 1), jnp.where(lane < DIM, tail, 0.0))
        for j in range(2):
            at = pl.ds(pl.multiple_of(j * ROWS + i * TOKENS, 8), TOKENS)
            part = slice(j * TOKENS, (j + 1) * TOKENS)
            q_ref[at, :] = q[part]
            k_ref[at, :] = k[part]
            v_ref[at, :] = v[part]
            g_ref[at, :] = g[part]
        return 0

    lax.fori_loop(0, GROUPS, one, 0)


def pack_grads(dq, dk, dv):
    lane = lanes_of(dq.shape[0])
    turned = pltpu.roll(dk, 72, 1)
    upper = jnp.where(lane < 72, dq, turned)
    lower = jnp.where(lane < 16, turned, pltpu.roll(dv, 16, 1))
    return upper, lower


def store_grads(upper_ref, lower_ref, out):
    def one(i, _):
        for n, ref in enumerate((upper_ref, lower_ref)):
            both = [
                ref[pl.ds(pl.multiple_of(j * ROWS + i * TOKENS, 8), TOKENS), :] for j in range(2)
            ]
            out[i, 48 * n : 48 * n + 48, :] = jnp.concatenate(both, axis=0).astype(BF16)
        return 0

    lax.fori_loop(0, GROUPS, one, 0)


def combine(m1, l1, s1, m2, l2, s2):
    top = jnp.maximum(m1, m2)
    a1 = jnp.exp(m1 - top)
    a2 = jnp.exp(m2 - top)
    mass = l1 * a1 + l2 * a2
    return a1 / mass, (s1 * a1 + s2 * a2) / mass


def kernel(
    q_in, k_in, v_in, g_in, bias_ref, dq_out, dk_out, dv_out,
    send, plane, spat, temp,
    qs, ks, vs, gs, qt, kt, vt, gt,
    e_s, d_s, p_s, sl_s, e_t, d_t,
    stat_s, stat_t, to_t, to_s, from_s, from_t,
    grad_s, grad_t, back_s, back_t, final, landed,
    z_send, z_recv, y_send, y_recv, x_send, x_recv,
    ts_send, ts_recv, st_send, st_recv,
    bx_send, bx_recv, by_send, by_recv, bz_send, bz_recv,
):
    tm = lax.axis_index("tm")
    tok = lax.axis_index("tok")
    x, zhi, core = lax.div(tm, 4), lax.rem(lax.div(tm, 2), 2), lax.rem(tm, 2)
    zlo, y = lax.div(tok, 4), lax.rem(tok, 4)
    z = zhi * 8 + zlo
    spot = x * 2 + core
    my_pair = x * 8 + lax.div(y, 2) * 4 + core * 2 + lax.rem(y, 2)
    my_group = y * 8 + spot

    def remote(src, dst, s_sem, r_sem, target):
        return pltpu.make_async_remote_copy(
            src_ref=src, dst_ref=dst, send_sem=s_sem, recv_sem=r_sem,
            device_id=target, device_id_type=pl.DeviceIdType.MESH,
        )

    def start(src, dst, s_sem, r_sem, target, here):
        @pl.when(here)
        def _():
            pltpu.make_async_copy(src, dst, r_sem).start()

        @pl.when(jnp.logical_not(here))
        def _():
            remote(src, dst, s_sem, r_sem, target).start()

    def arrived(ref, sem):
        pltpu.make_async_copy(ref, ref, sem).wait()

    def sent(ref, sem, here):
        @pl.when(jnp.logical_not(here))
        def _():
            pltpu.make_async_copy(ref, ref, sem).wait()

    barrier = pltpu.get_barrier_semaphore()

    def hail_line(d, _):
        pl.semaphore_signal(
            barrier, inc=1, device_id=device(x, lax.rem(z + d, 16), core, y),
            device_id_type=pl.DeviceIdType.MESH,
        )
        return 0

    lax.fori_loop(1, 16, hail_line, 0)
    place = y * 8 + spot

    def hail_plane(d, _):
        other = lax.rem(place + d, 32)
        there = lax.rem(other, 8)
        pl.semaphore_signal(
            barrier, inc=1,
            device_id=device(lax.div(there, 2), z, lax.rem(there, 2), lax.div(other, 8)),
            device_id_type=pl.DeviceIdType.MESH,
        )
        return 0

    lax.fori_loop(1, 32, hail_plane, 0)
    pack_heads((q_in, k_in, v_in, g_in), send)
    pl.semaphore_wait(barrier, 46)

    pltpu.make_async_copy(send.at[z], plane.at[z], z_recv.at[z]).start()

    def send_line(n, _):
        d = jnp.where(lax.rem(n, 2) == 1, lax.div(n + 1, 2), 16 - lax.div(n, 2))
        to = lax.rem(z + d, 16)
        remote(
            send.at[to], plane.at[z], z_send.at[to], z_recv.at[z], device(x, to, core, y)
        ).start()
        return 0

    lax.fori_loop(1, 16, send_line, 0)

    def forward(n, _):
        d = jnp.where(lax.rem(n, 2) == 1, 16 - lax.div(n + 1, 2), lax.div(n, 2))
        source = lax.rem(z + d, 16)
        hi, lo = lax.div(source, 8), lax.rem(source, 8)
        arrived(plane.at[source], z_recv.at[source])
        to_x, to_core = lax.div(lo, 2), lax.rem(lo, 2)
        start(
            plane.at[source], temp.at[4 * x + 2 * hi + core],
            x_send.at[source], x_recv.at[4 * x + 2 * hi + core],
            device(to_x, z, to_core, y), lo == spot,
        )
        for p in range(2):
            to_y = 2 * hi + p
            start(
                plane.at[source, p], spat.at[y * 8 + lo],
                y_send.at[2 * source + p], y_recv.at[y * 8 + lo],
                device(x, z, core, to_y), to_y == y,
            )
        return 0

    lax.fori_loop(0, 16, forward, 0)

    def wait_x(n, _):
        arrived(temp.at[n], x_recv.at[n])
        return 0

    lax.fori_loop(0, 16, wait_x, 0)
    unpack_blocks(
        lambda i, a, n: temp[lax.div(i, 2), lax.rem(i, 2), a : a + n, :], qt, kt, vt, gt
    )
    frame_k = lax.broadcasted_iota(jnp.int32, (64, 64), 0)
    frame_q = lax.broadcasted_iota(jnp.int32, (64, 64), 1)
    frame_k = 2 * lax.rem(frame_k, 32) + lax.div(frame_k, 32)
    frame_q = 2 * lax.rem(frame_q, 32) + lax.div(frame_q, 32)
    offset = frame_k - frame_q
    bias = jnp.full((64, 64), -jnp.inf, F32)
    for j in range(2 * BAND):
        o = j - BAND if j < BAND else j - BAND + 1
        bias = jnp.where(offset == o, bias_ref[z, j], bias)
    stat_t[...] = jnp.zeros_like(stat_t)
    for t in range(TOKENS):
        at = pl.ds(t, 64, stride=TOKENS)
        s = lax.dot_general(
            kt[at, :].astype(BF16), qt[at, :].astype(BF16), NT, preferred_element_type=F32
        ) * SCALE + bias
        d = lax.dot_general(
            vt[at, :].astype(BF16), gt[at, :].astype(BF16), NT, preferred_element_type=F32
        )
        top = jnp.max(s, axis=0, keepdims=True)
        e = jnp.exp(s - top)
        e_t[t] = e
        d_t[t] = d
        stat_t[t : t + 1, 0:64] = top
        stat_t[24 + t : 25 + t, 0:64] = jnp.sum(e, axis=0, keepdims=True)
        stat_t[48 + t : 49 + t, 0:64] = jnp.sum(e * d, axis=0, keepdims=True)
    turned = stat_t[...].T
    to_s[...] = jnp.zeros_like(to_s)
    for j in range(2):
        to_s[pl.ds(j, 32, stride=8), :] = turned[32 * j : 32 * j + 32]

    def send_ts(n, _):
        r = lax.rem(my_pair + n, 32)
        rx, rh, rc, rp = (
            lax.div(r, 8), lax.rem(lax.div(r, 4), 2), lax.rem(lax.div(r, 2), 2), lax.rem(r, 2),
        )
        start(
            to_s.at[pl.ds(pl.multiple_of(r * 8, 8), 8)],
            from_t.at[pl.ds(pl.multiple_of(my_group * 8, 8), 8)],
            ts_send.at[r], ts_recv.at[my_group], device(rx, z, rc, 2 * rh + rp), r == my_pair,
        )
        return 0

    lax.fori_loop(0, 32, send_ts, 0)

    def wait_y(n, _):
        arrived(spat.at[n], y_recv.at[n])
        return 0

    lax.fori_loop(0, 32, wait_y, 0)
    unpack_blocks(lambda i, a, n: spat[i, a : a + n, :], qs, ks, vs, gs)
    stat_s[...] = jnp.zeros_like(stat_s)

    def scores(n, _):
        j, b = lax.div(n, 3), lax.rem(n, 3)
        keys_at = pl.ds(pl.multiple_of(j * ROWS, 8), ROWS)
        rows_at = pl.ds(pl.multiple_of(j * ROWS + b * 256, 8), 256)
        lanes_at = pl.ds(pl.multiple_of(b * 256, 128), 256)
        s = lax.dot_general(
            ks[keys_at, :].astype(BF16), qs[rows_at, :].astype(BF16), NT,
            preferred_element_type=F32,
        ) * SCALE
        d = lax.dot_general(
            vs[keys_at, :].astype(BF16), gs[rows_at, :].astype(BF16), NT,
            preferred_element_type=F32,
        )
        top = jnp.max(s, axis=0, keepdims=True)
        e = jnp.exp(s - top)
        e_s[j, :, lanes_at] = e
        d_s[j, :, lanes_at] = d
        stat_s[pl.ds(j, 1), lanes_at] = top
        stat_s[pl.ds(2 + j, 1), lanes_at] = jnp.sum(e, axis=0, keepdims=True)
        stat_s[pl.ds(4 + j, 1), lanes_at] = jnp.sum(e * d, axis=0, keepdims=True)
        return 0

    lax.fori_loop(0, 6, scores, 0)
    stat = stat_s[...]
    row = lax.broadcasted_iota(jnp.int32, (256, ROWS), 0)
    lane = lax.broadcasted_iota(jnp.int32, (256, ROWS), 1)
    spread = jnp.where(
        lax.div(lane, TOKENS) == lax.div(row, 8), jnp.concatenate([stat] * 32, axis=0), 0.0
    )
    row = lax.broadcasted_iota(jnp.int32, (ROWS, 128), 0)
    lane = lax.broadcasted_iota(jnp.int32, (ROWS, 128), 1)
    pick = (lax.rem(row, TOKENS) == lane).astype(F32)
    to_t[...] = jnp.dot(
        spread, pick, precision=lax.Precision.HIGHEST, preferred_element_type=F32
    )

    def send_st(n, _):
        i = lax.rem(my_group + n, 32)
        iy, lo = lax.div(i, 8), lax.rem(i, 8)
        start(
            to_t.at[pl.ds(pl.multiple_of(i * 8, 8), 8)],
            from_s.at[pl.ds(pl.multiple_of(my_pair * 8, 8), 8)],
            st_send.at[i], st_recv.at[my_pair],
            device(lax.div(lo, 2), z, lax.rem(lo, 2), iy), i == my_group,
        )
        return 0

    lax.fori_loop(0, 32, send_st, 0)

    def wait_stats(n, _):
        at = pl.ds(pl.multiple_of(n * 8, 8), 8)
        arrived(from_t.at[at], ts_recv.at[n])
        arrived(from_s.at[at], st_recv.at[n])
        return 0

    lax.fori_loop(0, 32, wait_stats, 0)

    theirs = [
        jnp.concatenate(
            [from_s[pl.ds(2 * n + j, 32, stride=8), :] for j in range(2)], axis=0
        ).T[0:TOKENS]
        for n in range(3)
    ]
    mine = [stat_t[24 * n : 24 * n + 24, 0:64] for n in range(3)]
    scale_t, delta_t = combine(*mine, *theirs)
    for t in range(TOKENS):
        at = pl.ds(t, 64, stride=TOKENS)
        rounded = (e_t[t] * scale_t[t : t + 1]).astype(BF16)
        slope = (rounded.astype(F32) * (d_t[t] - delta_t[t : t + 1])).astype(BF16)
        k = kt[at, :].astype(BF16)
        q = qt[at, :].astype(BF16)
        g = gt[at, :].astype(BF16)
        dk = jnp.dot(slope, q, preferred_element_type=F32) * SCALE
        dv = jnp.dot(rounded, g, preferred_element_type=F32)
        across = slope.astype(F32).T.astype(BF16)
        dq = jnp.dot(across, k, preferred_element_type=F32) * SCALE
        upper, lower = pack_grads(dq, dk, dv)
        qt[at, :] = upper
        vt[at, :] = lower
    store_grads(qt, vt, grad_t)

    def send_bx(n, _):
        hi, place_x = lax.rem(n, 2), lax.rem(spot + lax.div(n, 2), 8)
        to_x, to_core = lax.div(place_x, 2), lax.rem(place_x, 2)
        block = pl.ds(pl.multiple_of(2 * (4 * to_x + 2 * hi + to_core), 2), 2)
        source = hi * 8 + spot
        start(
            grad_t.at[block], back_t.at[source],
            bx_send.at[hi * 8 + place_x], bx_recv.at[source],
            device(to_x, z, to_core, y), place_x == spot,
        )
        return 0

    lax.fori_loop(0, 16, send_bx, 0)

    lane = lax.broadcasted_iota(jnp.int32, (64, ROWS), 1)
    row = lax.broadcasted_iota(jnp.int32, (64, ROWS), 0)
    own = lax.div(lane, TOKENS) == lax.rem(row, 32)
    got = jnp.concatenate([from_t[pl.ds(j, 32, stride=8), :] for j in range(2)], axis=0)
    theirs = []
    lane = lax.broadcasted_iota(jnp.int32, (128, ROWS), 1)
    row = lax.broadcasted_iota(jnp.int32, (128, ROWS), 0)
    for n in range(3):
        repeat = (lax.rem(lane, TOKENS) == row - TOKENS * n).astype(F32)
        wide = jnp.dot(
            got, repeat, precision=lax.Precision.HIGHEST, preferred_element_type=F32
        )
        wide = jnp.where(own, wide, 0.0)
        theirs.append(
            jnp.concatenate(
                [jnp.sum(wide[32 * j : 32 * j + 32], axis=0, keepdims=True) for j in range(2)],
                axis=0,
            )
        )
    mine = [stat[2 * n : 2 * n + 2] for n in range(3)]
    scale_s, delta_s = combine(*mine, *theirs)
    stat_s[0:2, :] = scale_s
    stat_s[2:4, :] = delta_s

    def slopes(n, _):
        j, b = lax.div(n, 3), lax.rem(n, 3)
        lanes_at = pl.ds(pl.multiple_of(b * 256, 128), 256)
        rounded = (e_s[j, :, lanes_at] * stat_s[pl.ds(j, 1), lanes_at]).astype(BF16)
        gap = d_s[j, :, lanes_at] - stat_s[pl.ds(2 + j, 1), lanes_at]
        p_s[j, :, lanes_at] = rounded
        sl_s[j, :, lanes_at] = (rounded.astype(F32) * gap).astype(BF16)
        return 0

    lax.fori_loop(0, 6, slopes, 0)

    def grads(j, _):
        rows_at = pl.ds(pl.multiple_of(j * ROWS, 8), ROWS)
        q = qs[rows_at, :].astype(BF16)
        g = gs[rows_at, :].astype(BF16)
        k_turned = ks[rows_at, :].T.astype(BF16)
        dk = jnp.dot(sl_s[j], q, preferred_element_type=F32) * SCALE
        dv = jnp.dot(p_s[j], g, preferred_element_type=F32)
        dq = jnp.dot(k_turned, sl_s[j], preferred_element_type=F32).T * SCALE
        upper, lower = pack_grads(dq, dk, dv)
        qs[rows_at, :] = upper
        vs[rows_at, :] = lower
        return 0

    lax.fori_loop(0, 2, grads, 0)
    store_grads(qs, vs, grad_s)

    def send_by(n, _):
        to_y = lax.rem(y + n, 4)
        start(
            grad_s.at[pl.ds(pl.multiple_of(to_y * 8, 8), 8)], back_s.at[y],
            by_send.at[to_y], by_recv.at[y], device(x, z, core, to_y), to_y == y,
        )
        return 0

    lax.fori_loop(0, 4, send_by, 0)

    def wait_bx(n, _):
        arrived(back_t.at[n], bx_recv.at[n])
        return 0

    lax.fori_loop(0, 16, wait_bx, 0)

    def wait_by(n, _):
        arrived(back_s.at[n], by_recv.at[n])
        return 0

    lax.fori_loop(0, 4, wait_by, 0)

    def send_home(n, _):
        d = jnp.where(lax.rem(n, 2) == 1, lax.div(n + 1, 2), 16 - lax.div(n, 2))
        to = lax.rem(z + d, 16)
        hi, lo = lax.div(to, 8), lax.rem(to, 8)
        for p in range(2):
            total = back_s[2 * hi + p, lo].astype(F32) + back_t[to, p].astype(F32)
            final[to, p] = total.astype(BF16)
        start(
            final.at[to], landed.at[z], bz_send.at[to], bz_recv.at[z],
            device(x, to, core, y), to == z,
        )
        return 0

    lax.fori_loop(0, 16, send_home, 0)

    def wait_home(n, _):
        arrived(landed.at[n], bz_recv.at[n])
        return 0

    lax.fori_loop(0, 16, wait_home, 0)

    def restore(pair, _):
        lane = lanes_of(PAIR)
        runs = [[[] for _ in range(WIDTH // 128)] for _ in range(3)]
        for head in range(HEADS):
            upper = landed[head, pair, 0:48, :].astype(F32)
            lower = landed[head, pair, 48:96, :].astype(F32)
            start_lane = head * DIM
            for array, value, source, first, width in (
                (0, upper, 0, 0, 72), (1, upper, 72, 0, 56), (1, lower, 0, 56, 16),
                (2, lower, 16, 0, 72),
            ):
                target = start_lane + first
                while width:
                    step = min(width, 128 - target % 128)
                    low = target % 128
                    runs[array][target // 128].append(
                        (value, (low - source) % 128, low, low + step)
                    )
                    source, target, width = source + step, target + step, width - step
        for array, out in enumerate((dq_out, dk_out, dv_out)):
            for t in range(WIDTH // 128):
                whole = assemble(lane, runs[array][t])
                for j in range(2):
                    out[2 * pair + j, :, 128 * t : 128 * t + 128] = whole[
                        TOKENS * j : TOKENS * j + TOKENS
                    ].astype(BF16)
        return 0

    lax.fori_loop(0, 2, restore, 0)

    def drain(n, _):
        @pl.when(n != z)
        def _():
            pltpu.make_async_copy(send.at[n], send.at[n], z_send.at[n]).wait()
            pltpu.make_async_copy(final.at[n], final.at[n], bz_send.at[n]).wait()

        hi, lo = lax.div(n, 8), lax.rem(n, 8)
        sent(plane.at[n], x_send.at[n], lo == spot)
        sent(back_t.at[n], bx_send.at[n], lo == spot)
        for p in range(2):
            sent(plane.at[n, p], y_send.at[2 * n + p], 2 * hi + p == y)
        return 0

    lax.fori_loop(0, 16, drain, 0)

    def drain_stats(n, _):
        at = pl.ds(pl.multiple_of(n * 8, 8), 8)
        sent(to_s.at[at], ts_send.at[n], n == my_pair)
        sent(to_t.at[at], st_send.at[n], n == my_group)
        return 0

    lax.fori_loop(0, 32, drain_stats, 0)

    def drain_y(n, _):
        sent(back_s.at[n], by_send.at[n], n == y)
        return 0

    lax.fori_loop(0, 4, drain_y, 0)


def body(queries, keys, values, out_grad, time_bias):
    vmem = pl.BlockSpec(memory_space=pltpu.VMEM)
    shape = jax.ShapeDtypeStruct(queries.shape, BF16)
    wide = pltpu.VMEM((2 * ROWS, 128), F32)
    dma = pltpu.SemaphoreType.DMA
    return pl.pallas_call(
        kernel,
        out_shape=(shape, shape, shape),
        in_specs=[vmem] * 4 + [pl.BlockSpec(memory_space=pltpu.SMEM)],
        out_specs=(vmem, vmem, vmem),
        scratch_shapes=[
            pltpu.VMEM((16, 2, FWD, 128), BF16),
            pltpu.VMEM((16, 2, FWD, 128), BF16),
            pltpu.VMEM((32, FWD, 128), BF16),
            pltpu.VMEM((16, 2, FWD, 128), BF16),
            wide, wide, wide, wide, wide, wide, wide, wide,
            pltpu.VMEM((2, ROWS, ROWS), F32),
            pltpu.VMEM((2, ROWS, ROWS), F32),
            pltpu.VMEM((2, ROWS, ROWS), BF16),
            pltpu.VMEM((2, ROWS, ROWS), BF16),
            pltpu.VMEM((TOKENS, 64, 64), F32),
            pltpu.VMEM((TOKENS, 64, 64), F32),
            pltpu.VMEM((8, ROWS), F32),
            pltpu.VMEM((128, 128), F32),
            pltpu.VMEM((256, 128), F32),
            pltpu.VMEM((256, 128), F32),
            pltpu.VMEM((256, 128), F32),
            pltpu.VMEM((256, 128), F32),
            pltpu.VMEM((32, BWD, 128), BF16),
            pltpu.VMEM((32, BWD, 128), BF16),
            pltpu.VMEM((4, 8, BWD, 128), BF16),
            pltpu.VMEM((16, 2, BWD, 128), BF16),
            pltpu.VMEM((16, 2, BWD, 128), BF16),
            pltpu.VMEM((16, 2, BWD, 128), BF16),
            dma((16,)), dma((16,)), dma((32,)), dma((32,)), dma((16,)), dma((16,)),
            dma((32,)), dma((32,)), dma((32,)), dma((32,)),
            dma((16,)), dma((16,)), dma((4,)), dma((4,)), dma((16,)), dma((16,)),
        ],
        compiler_params=pltpu.CompilerParams(
            collective_id=0, has_side_effects=True, vmem_limit_bytes=56 * 2**20
        ),
    )(queries, keys, values, out_grad, time_bias)


def solution(mesh):
    spec = P("tm", "tok", None)
    return jax.shard_map(
        body, mesh=mesh, in_specs=(spec, spec, spec, spec, P()),
        out_specs=(spec, spec, spec), check_vma=False,
    )
```

time: 822 us -> 150 us (0.18)
  the two profiles are of different devices: /device:TPU:35 before, /device:TPU:1 now
where the time goes in v1:
time: 150 us; the launch traced here: 148 us
  Pallas kernels  144 us (96%)
  local copies, waits for them, and re-layouts  3.38 us (2%)
    pallas_call x1, Pallas kernels, body(): pl.pallas_call(kernel, out_shape=(shape, shape, shape), in_specs=[vmem] *...  144 us
    unnamed x7, local copies, waits for them, and re-layouts  3.38 us

profile of v1, /device:TPU:1, one launch (start us, length us, event | category | flops | bytes accessed | tf_op | source)
XLA Modules:
  0.0 147.8 jit_solution(11952182193236805184)
XLA Ops:
  0.6 143.8 %shard_map.76 = (bf16[4,24,1152]{2,1,0:T(8,128)(2,1)}, bf16[4,24,1152]{2,1,0:T(8,128)(2,1)}, bf16[4,24,1152]{2,1,0:T(8,128)(2,1)}) custom-call(bf16[4,24,1152]{2,1,0:T(8,128)(2,1)} %q_in.1, bf16[4,24,1152]{2,1,0:T(8,128)(2,1)} %k_in.1, bf16[4,24,1152]{2,1,0:T(8,128)(2,1)} %v_in.1, bf16[4,24,1152]{2,1,0:T(8,128)(2,1)} %g_in.1, f32[16,16]{1,0:T(8,128)} %bias_ref.1), custom_call_target="tpu_custom_call" | custom-call | tf_op jit(solution)/shard_map/pallas_call | solution.py:562
  144.5 0.0 copy-start.1
  144.5 1.7 %copy.11 = bf16[4,24,1152]{2,1,0:T(8,128)(2,1)} copy(bf16[4,24,1152]{2,1,0:T(8,128)(2,1)} %get-tuple-element.6) | data formatting | bytes 442368
  146.1 0.0 copy-done.1
  146.1 0.0 copy-start
  146.1 0.7 copy.12
  146.8 0.3 copy-done
  147.2 0.7 copy.13
Async XLA Ops:
  144.5 1.7 %copy-start.1 = (bf16[4,24,1152]{2,1,0:T(8,128)(2,1)S(1)}, bf16[4,24,1152]{2,1,0:T(8,128)(2,1)}, u32[]{:S(2)}) copy-start(bf16[4,24,1152]{2,1,0:T(8,128)(2,1)} %get-tuple-element.7) | copy-start | bytes 663556
  146.1 1.0 copy-start

commit v2 on v0

v2 whole, which is shorter than its diff:
```python
import jax
import jax.numpy as jnp
from jax import lax
from jax.experimental import pallas as pl
from jax.experimental.pallas import tpu as pltpu
from jax.sharding import PartitionSpec as P

F32 = jnp.float32
BF16 = jnp.bfloat16
HEADS = 16
DIM = 72
TOKENS = 24
WIDTH = HEADS * DIM
BAND = 8
GROUPS = 32
ROWS = GROUPS * TOKENS
PAIR = 2 * TOKENS
SCALE = DIM**-0.5
NT = (((1,), (1,)), ((), ()))
HIGHEST = lax.Precision.HIGHEST


def device(x, z, core, y):
    return (x * 4 + lax.div(z, 8) * 2 + core, lax.rem(z, 8) * 4 + y)


def lanes_of(rows):
    return lax.broadcasted_iota(jnp.int32, (rows, 128), 1)


def turn(value, shift):
    if isinstance(shift, int):
        shift %= 128
        return value if shift == 0 else pltpu.roll(value, shift, 1)
    return pltpu.roll(value, lax.rem(shift + 256, 128), 1)


def group(value, r):
    return value[16 * r : 16 * r + 16]


def head_run(ref, pair, head):
    first, offset = head * DIM // 128, head * DIM % 128
    tile = [
        jnp.concatenate(
            [ref[2 * pair + j, :, 128 * t : 128 * t + 128].astype(F32) for j in range(2)], axis=0
        )
        for t in range(first, first + (2 if offset + DIM > 128 else 1))
    ]
    if len(tile) == 1:
        return tile[0], offset
    return jnp.where(lanes_of(PAIR) >= offset, tile[0], tile[1]), offset


def pack_first(q_in, k_in, out):
    lane, lane16 = lanes_of(PAIR), lanes_of(16)
    for head in range(HEADS):
        extra = None
        for pair in range(2):
            q, at = head_run(q_in, pair, head)
            k, _ = head_run(k_in, pair, head)
            k = turn(k, 72 - at)
            main = jnp.where(lane < DIM, turn(q, -at), k).astype(BF16)
            for r in range(3):
                out[head, 4 * pair + r] = group(main, r)
                low = 16 * (3 * pair + r)
                piece = turn(group(k, r), low)
                extra = piece if extra is None else jnp.where(lane16 >= low, piece, extra)
        out[head, 3] = extra.astype(BF16)


def pack_second(g_in, v_in, out_g, out_v):
    lane16 = lanes_of(16)
    half = lane16 < 64
    for head in range(HEADS):
        extra = None
        shared_g, shared_v = [], []
        for pair in range(2):
            g, at = head_run(g_in, pair, head)
            v, _ = head_run(v_in, pair, head)
            g = turn(g, -at)
            v = turn(v, -at - 8)
            out_g[head, 3 * pair] = jnp.where(half, group(g, 0), turn(group(g, 1), 64)).astype(BF16)
            out_v[head, 2 * pair] = jnp.where(half, group(v, 0), turn(group(v, 1), 64)).astype(BF16)
            shared_g.append(group(g, 2))
            shared_v.append(group(v, 2))
            for r in range(3):
                low = 16 * (3 * pair + r)
                piece = turn(group(g, r), low - 64)
                extra = piece if extra is None else jnp.where(lane16 >= low, piece, extra)
                extra = jnp.where(lane16 >= low + 8, turn(group(v, r), low + 16), extra)
        out_g[head, 1] = jnp.where(half, shared_g[0], turn(shared_g[1], 64)).astype(BF16)
        out_v[head, 1] = jnp.where(half, shared_v[0], turn(shared_v[1], 64)).astype(BF16)
        out_g[head, 2] = extra.astype(BF16)


def store_rows(ref, i, value):
    for j in range(2):
        at = pl.ds(pl.multiple_of(j * ROWS + i * TOKENS, 8), TOKENS)
        ref[at, :] = value[j * TOKENS : (j + 1) * TOKENS]


def load_rows(ref, i):
    return jnp.concatenate(
        [
            ref[pl.ds(pl.multiple_of(j * ROWS + i * TOKENS, 8), TOKENS), :]
            for j in range(2)
        ],
        axis=0,
    )


def unpack_first(tile, pair_of, q_ref, k_ref):
    def one(i, _):
        lane = lanes_of(PAIR)
        p = pair_of(i)
        main = jnp.concatenate([tile(i, r + p).astype(F32) for r in range(3)], axis=0)
        extra = tile(i, 3 - 3 * p).astype(F32)
        extra = jnp.concatenate([turn(extra, -48 * p - 16 * r) for r in range(3)], axis=0)
        store_rows(q_ref, i, jnp.where(lane < DIM, main, 0.0))
        store_rows(k_ref, i, turn(jnp.where(lane >= DIM, main, extra), 56))
        return 0

    lax.fori_loop(0, GROUPS, one, 0)


def unpack_second(tile, pair_of, g_ref):
    def one(i, _):
        lane = lanes_of(PAIR)
        p = pair_of(i)
        own = tile(i, 2 * p).astype(F32)
        shared = tile(i, 1 - p).astype(F32)
        extra = tile(i, 2 - p).astype(F32)
        main = jnp.concatenate([own, turn(own, 64), turn(shared, 64 * p)], axis=0)
        tail = jnp.concatenate([turn(extra, 64 - 48 * p - 16 * r) for r in range(3)], axis=0)
        store_rows(g_ref, i, jnp.where(lane < 64, main, jnp.where(lane < DIM, tail, 0.0)))
        return 0

    lax.fori_loop(0, GROUPS, one, 0)


def unpack_third(tile, tile_g, pair_of, v_ref):
    def one(i, _):
        lane = lanes_of(PAIR)
        p = pair_of(i)
        own = tile(i, p).astype(F32)
        shared = tile(i, 1 - p).astype(F32)
        extra = tile_g(i, 2 - p).astype(F32)
        main = jnp.concatenate([turn(own, 8), turn(own, 72), turn(shared, 8 - 64 * p)], axis=0)
        head = jnp.concatenate([turn(extra, -8 - 48 * p - 16 * r) for r in range(3)], axis=0)
        store_rows(v_ref, i, jnp.where(lane < 8, head, jnp.where(lane < DIM, main, 0.0)))
        return 0

    lax.fori_loop(0, GROUPS, one, 0)


def value_tiles(dv, p):
    lane16 = lanes_of(16)
    half = lane16 < 64
    own = jnp.where(half, group(dv, 0), turn(group(dv, 1), 64))
    shared = turn(jnp.where(half, group(dv, 2), 0.0), 64 * p)
    extra = jnp.zeros_like(own)
    for r in reversed(range(3)):
        inside = (lane16 >= 16 * r) & (lane16 < 16 * r + 8)
        extra = jnp.where(inside, turn(group(dv, r), 16 * r - 64), extra)
    return own, shared, turn(extra, 48 * p)


def key_tiles(dq, dk, p):
    lane, lane16 = lanes_of(PAIR), lanes_of(16)
    dk = turn(dk, 72)
    main = jnp.where(lane < DIM, dq, dk)
    extra = jnp.zeros((16, 128), F32)
    for r in range(3):
        inside = (lane16 >= 16 * r) & (lane16 < 16 * r + 16)
        extra = jnp.where(inside, turn(group(dk, r), 16 * r), extra)
    return [group(main, r) for r in range(3)], turn(extra, 48 * p)


def spread_heads(parts, out, pair):
    lane = lanes_of(PAIR)
    for t in range(WIDTH // 128):
        whole = None
        for head in reversed(range(HEADS)):
            low, high = head * DIM - 128 * t, head * DIM + DIM - 128 * t
            if high <= 0 or low >= 128:
                continue
            whole = parts[head] if whole is None else jnp.where(lane < high, parts[head], whole)
        for j in range(2):
            out[2 * pair + j, :, 128 * t : 128 * t + 128] = whole[
                TOKENS * j : TOKENS * j + TOKENS
            ].astype(BF16)


def restore_values(landed, dv_out):
    for pair in range(2):
        parts = []
        lane = lanes_of(PAIR)
        for head in range(HEADS):
            own = landed[head, 3 * pair].astype(F32)
            shared = landed[head, 1].astype(F32)
            extra = landed[head, 2].astype(F32)
            main = jnp.concatenate([own, turn(own, 64), turn(shared, 64 * pair)], axis=0)
            tail = jnp.concatenate(
                [turn(extra, 64 - 48 * pair - 16 * r) for r in range(3)], axis=0
            )
            parts.append(turn(jnp.where(lane < 64, main, tail), head * DIM))
        spread_heads(parts, dv_out, pair)


def restore_keys(landed, dq_out, dk_out):
    for pair in range(2):
        lane = lanes_of(PAIR)
        q_parts, k_parts = [], []
        for head in range(HEADS):
            main = jnp.concatenate(
                [landed[head, 4 * pair + r].astype(F32) for r in range(3)], axis=0
            )
            extra = landed[head, 3].astype(F32)
            extra = jnp.concatenate([turn(extra, -48 * pair - 16 * r) for r in range(3)], axis=0)
            q_parts.append(turn(main, head * DIM))
            k_parts.append(turn(jnp.where(lane >= DIM, main, extra), head * DIM - DIM))
        spread_heads(q_parts, dq_out, pair)
        spread_heads(k_parts, dk_out, pair)


def far_step(n):
    return jnp.where(lax.rem(n, 2) == 1, 8 + lax.div(n, 2), 8 - lax.div(n, 2))


def scratch():
    dma = pltpu.SemaphoreType.DMA

    def tiles(blocks, count):
        return pltpu.VMEM((blocks, count, 16, 128), BF16)

    wide = pltpu.VMEM((2 * ROWS, 128), F32)
    square = (2, ROWS, ROWS)
    small = (TOKENS, 64, 64)
    shapes = {}
    for n, (whole, part) in {1: (7, 4), 2: (4, 3), 3: (3, 2)}.items():
        shapes[f"send{n}"] = tiles(16, whole)
        shapes[f"plane{n}"] = tiles(16, whole)
        shapes[f"temp{n}"] = tiles(16, whole)
        shapes[f"spat{n}"] = tiles(32, part)
        for name, count in (("zs", 16), ("zr", 16), ("xs", 16), ("xr", 16), ("ys", 32), ("yr", 32)):
            shapes[f"{name}{n}"] = dma((count,))
    for n, (whole, part) in {"v": (4, 3), "k": (7, 4)}.items():
        shapes[f"grad_t{n}"] = tiles(16, whole)
        shapes[f"back_t{n}"] = tiles(16, whole)
        shapes[f"final{n}"] = tiles(16, whole)
        shapes[f"landed{n}"] = tiles(16, whole)
        shapes[f"grad_s{n}"] = tiles(32, part)
        shapes[f"back_s{n}"] = tiles(32, part)
        for name, count in (
            ("bxs", 16), ("bxr", 16), ("bys", 32), ("byr", 32), ("bzs", 16), ("bzr", 16),
        ):
            shapes[f"{name}{n}"] = dma((count,))
    for name in ("qs", "ks", "vs", "gs", "qt", "kt", "vt", "gt"):
        shapes[name] = wide
    shapes.update(
        e_s=pltpu.VMEM(square, F32), d_s=pltpu.VMEM(square, F32),
        p_s=pltpu.VMEM(square, BF16), sl_s=pltpu.VMEM(square, BF16),
        e_t=pltpu.VMEM(small, F32), d_t=pltpu.VMEM(small, F32), p_t=pltpu.VMEM(small, BF16),
        stat_s=pltpu.VMEM((2, 8, ROWS), F32), scale_s=pltpu.VMEM((8, ROWS), F32),
        stat_t=pltpu.VMEM((2, 128, 128), F32),
    )
    for n in ("a", "b"):
        for name in ("to_s", "to_t", "from_s", "from_t"):
            shapes[name + n] = pltpu.VMEM((256, 128), F32)
        for name in ("tss", "tsr", "sts", "str"):
            shapes[name + n] = dma((32,))
    return shapes


def kernel(names, q_in, k_in, v_in, g_in, bias_ref, dq_out, dk_out, dv_out, *refs):
    m = dict(zip(names, refs, strict=True))
    tm = lax.axis_index("tm")
    tok = lax.axis_index("tok")
    x, zhi, core = lax.div(tm, 4), lax.rem(lax.div(tm, 2), 2), lax.rem(tm, 2)
    zlo, y = lax.div(tok, 4), lax.rem(tok, 4)
    z = zhi * 8 + zlo
    spot = x * 2 + core
    my_p = lax.rem(y, 2)
    my_pair = x * 8 + lax.div(y, 2) * 4 + core * 2 + my_p
    my_group = y * 8 + spot

    def remote(src, dst, s_sem, r_sem, target):
        return pltpu.make_async_remote_copy(
            src_ref=src, dst_ref=dst, send_sem=s_sem, recv_sem=r_sem,
            device_id=target, device_id_type=pl.DeviceIdType.MESH,
        )

    def start(src, dst, s_sem, r_sem, target, here):
        @pl.when(here)
        def _():
            pltpu.make_async_copy(src, dst, r_sem).start()

        @pl.when(jnp.logical_not(here))
        def _():
            remote(src, dst, s_sem, r_sem, target).start()

    def arrived(ref, sem):
        pltpu.make_async_copy(ref, ref, sem).wait()

    def sent(ref, sem, here):
        @pl.when(jnp.logical_not(here))
        def _():
            pltpu.make_async_copy(ref, ref, sem).wait()

    def loop(low, high, step):
        def one(n, _):
            step(n)
            return 0

        lax.fori_loop(low, high, one, 0)

    barrier = pltpu.get_barrier_semaphore()

    def hail(target):
        pl.semaphore_signal(
            barrier, inc=1, device_id=target, device_id_type=pl.DeviceIdType.MESH
        )

    loop(1, 16, lambda n: hail(device(x, lax.rem(z + far_step(n), 16), core, y)))

    def hail_plane(n):
        other = lax.rem(my_group + n, 32)
        there = lax.rem(other, 8)
        hail(device(lax.div(there, 2), z, lax.rem(there, 2), lax.div(other, 8)))

    loop(1, 32, hail_plane)

    def send_line(c):
        send, plane = m[f"send{c}"], m[f"plane{c}"]

        def one(n):
            to = lax.rem(z + far_step(n), 16)
            start(
                send.at[to], plane.at[z], m[f"zs{c}"].at[to], m[f"zr{c}"].at[z],
                device(x, to, core, y), to == z,
            )

        loop(1, 17, one)

    pack_first(q_in, k_in, m["send1"])
    pl.semaphore_wait(barrier, 46)
    send_line(1)
    pack_second(g_in, v_in, m["send2"], m["send3"])
    send_line(2)
    send_line(3)

    def forward(c, shift, part):
        plane, temp, spat = m[f"plane{c}"], m[f"temp{c}"], m[f"spat{c}"]

        def one(n):
            source = lax.rem(z + 16 - far_step(n), 16)
            hi, lo = lax.div(source, 8), lax.rem(source, 8)
            arrived(plane.at[source], m[f"zr{c}"].at[source])
            to_x, to_core = lax.div(lo, 2), lax.rem(lo, 2)
            slot = 4 * x + 2 * hi + core
            start(
                plane.at[source], temp.at[slot], m[f"xs{c}"].at[source], m[f"xr{c}"].at[slot],
                device(to_x, z, to_core, y), lo == spot,
            )
            for p in range(2):
                to_y = 2 * hi + p
                start(
                    plane.at[source, pl.ds(shift * p, part)], spat.at[y * 8 + lo],
                    m[f"ys{c}"].at[2 * source + p], m[f"yr{c}"].at[y * 8 + lo],
                    device(x, z, core, to_y), to_y == y,
                )

        loop(1, 17, one)

    def wait_x(c):
        loop(0, 16, lambda n: arrived(m[f"temp{c}"].at[n], m[f"xr{c}"].at[n]))

    def wait_y(c):
        loop(0, 32, lambda n: arrived(m[f"spat{c}"].at[n], m[f"yr{c}"].at[n]))

    def temp_tile(c, shift):
        return lambda i, t: m[f"temp{c}"][lax.div(i, 2), t + shift * lax.rem(i, 2)]

    def spat_tile(c):
        return lambda i, t: m[f"spat{c}"][i, t]

    def temp_pair(i):
        return lax.rem(i, 2)

    def spat_pair(i):
        return my_p

    def send_ts(c):
        to_s, from_t = m["to_s" + c], m["from_t" + c]
        turned = m["stat_t"][0 if c == "a" else 1].T
        to_s[...] = jnp.zeros_like(to_s)
        for j in range(2):
            to_s[pl.ds(j, 32, stride=8), :] = turned[32 * j : 32 * j + 32]

        def one(n):
            r = lax.rem(my_pair + n, 32)
            to_y = 2 * lax.rem(lax.div(r, 4), 2) + lax.rem(r, 2)
            start(
                to_s.at[pl.ds(pl.multiple_of(r * 8, 8), 8)],
                from_t.at[pl.ds(pl.multiple_of(my_group * 8, 8), 8)],
                m["tss" + c].at[r], m["tsr" + c].at[my_group],
                device(lax.div(r, 8), z, lax.rem(lax.div(r, 2), 2), to_y), r == my_pair,
            )

        loop(0, 32, one)

    def send_st(c):
        to_t, from_s = m["to_t" + c], m["from_s" + c]
        stat = m["stat_s"][0 if c == "a" else 1]
        row = lax.broadcasted_iota(jnp.int32, (256, ROWS), 0)
        lane = lax.broadcasted_iota(jnp.int32, (256, ROWS), 1)
        own = lax.div(lane, TOKENS) == lax.div(row, 8)
        spread = jnp.where(own, jnp.concatenate([stat] * 32, axis=0), 0.0)
        row = lax.broadcasted_iota(jnp.int32, (ROWS, 128), 0)
        lane = lax.broadcasted_iota(jnp.int32, (ROWS, 128), 1)
        pick = (lax.rem(row, TOKENS) == lane).astype(F32)
        to_t[...] = jnp.dot(spread, pick, precision=HIGHEST, preferred_element_type=F32)

        def one(n):
            i = lax.rem(my_group + n, 32)
            lo = lax.rem(i, 8)
            start(
                to_t.at[pl.ds(pl.multiple_of(i * 8, 8), 8)],
                from_s.at[pl.ds(pl.multiple_of(my_pair * 8, 8), 8)],
                m["sts" + c].at[i], m["str" + c].at[my_pair],
                device(lax.div(lo, 2), z, lax.rem(lo, 2), lax.div(i, 8)), i == my_group,
            )

        loop(0, 32, one)

    def got_s(c, count):
        from_s = m["from_s" + c]

        def one(n):
            arrived(from_s.at[pl.ds(pl.multiple_of(n * 8, 8), 8)], m["str" + c].at[n])

        loop(0, 32, one)
        return [
            jnp.concatenate(
                [from_s[pl.ds(2 * n + j, 32, stride=8), :] for j in range(2)], axis=0
            ).T[0:TOKENS]
            for n in range(count)
        ]

    def got_t(c, count):
        from_t = m["from_t" + c]

        def one(n):
            arrived(from_t.at[pl.ds(pl.multiple_of(n * 8, 8), 8)], m["tsr" + c].at[n])

        loop(0, 32, one)
        lane = lax.broadcasted_iota(jnp.int32, (64, ROWS), 1)
        row = lax.broadcasted_iota(jnp.int32, (64, ROWS), 0)
        own = lax.div(lane, TOKENS) == lax.rem(row, 32)
        got = jnp.concatenate([from_t[pl.ds(j, 32, stride=8), :] for j in range(2)], axis=0)
        lane = lax.broadcasted_iota(jnp.int32, (128, ROWS), 1)
        row = lax.broadcasted_iota(jnp.int32, (128, ROWS), 0)
        found = []
        for n in range(count):
            repeat = (lax.rem(lane, TOKENS) == row - TOKENS * n).astype(F32)
            wide = jnp.dot(got, repeat, precision=HIGHEST, preferred_element_type=F32)
            wide = jnp.where(own, wide, 0.0)
            found.append(
                jnp.concatenate(
                    [jnp.sum(wide[32 * j : 32 * j + 32], axis=0, keepdims=True) for j in range(2)],
                    axis=0,
                )
            )
        return found

    def scales(m1, l1, m2, l2):
        top = jnp.maximum(m1, m2)
        a1, a2 = jnp.exp(m1 - top), jnp.exp(m2 - top)
        mass = l1 * a1 + l2 * a2
        return a1 / mass, a2 / mass

    def return_x(c):
        grad, back = m["grad_t" + c], m["back_t" + c]

        def one(n):
            hi, there = lax.rem(n, 2), lax.rem(spot + lax.div(n, 2), 8)
            to_x, to_core = lax.div(there, 2), lax.rem(there, 2)
            source = hi * 8 + spot
            start(
                grad.at[4 * to_x + 2 * hi + to_core], back.at[source],
                m["bxs" + c].at[hi * 8 + there], m["bxr" + c].at[source],
                device(to_x, z, to_core, y), there == spot,
            )

        loop(0, 16, one)

    def return_y(c):
        grad, back = m["grad_s" + c], m["back_s" + c]

        def one(n):
            lo = lax.rem(zlo + far_step(lax.div(n, 4) + 1), 8)
            to_y = lax.rem(y + lax.rem(n, 4), 4)
            start(
                grad.at[to_y * 8 + lo], back.at[y * 8 + lo],
                m["bys" + c].at[to_y * 8 + lo], m["byr" + c].at[y * 8 + lo],
                device(x, z, core, to_y), to_y == y,
            )

        loop(0, 32, one)

    def go_home(c, whole, shift, part):
        back_s, back_t, final = m["back_s" + c], m["back_t" + c], m["final" + c]

        def one(n):
            to = lax.rem(z + far_step(n), 16)
            hi, lo = lax.div(to, 8), lax.rem(to, 8)
            arrived(back_t.at[to], m["bxr" + c].at[to])
            for p in range(2):
                slot = (2 * hi + p) * 8 + lo
                arrived(back_s.at[slot], m["byr" + c].at[slot])
            for t in range(whole):
                total = back_t[to, t].astype(F32)
                for p in range(2):
                    if 0 <= t - shift * p < part:
                        total = total + back_s[(2 * hi + p) * 8 + lo, t - shift * p].astype(F32)
                final[to, t] = total.astype(BF16)
            start(
                final.at[to], m["landed" + c].at[z], m["bzs" + c].at[to], m["bzr" + c].at[z],
                device(x, to, core, y), to == z,
            )

        loop(1, 17, one)

    def wait_home(c):
        loop(0, 16, lambda n: arrived(m["landed" + c].at[n], m["bzr" + c].at[n]))

    def drain(c):
        def one(n):
            hi, lo = lax.div(n, 8), lax.rem(n, 8)
            sent(m[f"send{c}"].at[n], m[f"zs{c}"].at[n], n == z)
            sent(m[f"plane{c}"].at[n], m[f"xs{c}"].at[n], lo == spot)
            for p in range(2):
                sent(m[f"spat{c}"].at[n], m[f"ys{c}"].at[2 * n + p], 2 * hi + p == y)

        loop(0, 16, one)

    def drain_back(c):
        def one(n):
            sent(m["final" + c].at[n], m["bzs" + c].at[n], n == z)
            sent(m["grad_t" + c].at[n], m["bxs" + c].at[n], lax.rem(n, 8) == spot)

        loop(0, 16, one)
        loop(
            0, 32,
            lambda n: sent(m["grad_s" + c].at[n], m["bys" + c].at[n], lax.div(n, 8) == y),
        )

    def drain_stats(c):
        def one(n):
            at = pl.ds(pl.multiple_of(n * 8, 8), 8)
            sent(m["to_s" + c].at[at], m["tss" + c].at[n], n == my_pair)
            sent(m["to_t" + c].at[at], m["sts" + c].at[n], n == my_group)

        loop(0, 32, one)

    qs, ks, vs, gs = m["qs"], m["ks"], m["vs"], m["gs"]
    qt, kt, vt, gt = m["qt"], m["kt"], m["vt"], m["gt"]
    e_s, d_s, p_s, sl_s = m["e_s"], m["d_s"], m["p_s"], m["sl_s"]
    e_t, d_t, p_t = m["e_t"], m["d_t"], m["p_t"]
    stat_s, stat_t, scale_s = m["stat_s"], m["stat_t"], m["scale_s"]
    stat_s[...] = jnp.zeros_like(stat_s)
    stat_t[...] = jnp.zeros_like(stat_t)

    forward(1, 3, 4)
    wait_x(1)
    unpack_first(temp_tile(1, 3), temp_pair, qt, kt)
    frame_k = lax.broadcasted_iota(jnp.int32, (64, 64), 0)
    frame_q = lax.broadcasted_iota(jnp.int32, (64, 64), 1)
    frame_k = 2 * lax.rem(frame_k, 32) + lax.div(frame_k, 32)
    frame_q = 2 * lax.rem(frame_q, 32) + lax.div(frame_q, 32)
    bias = jnp.full((64, 64), -jnp.inf, F32)
    for j in range(2 * BAND):
        o = j - BAND if j < BAND else j - BAND + 1
        bias = jnp.where(frame_k - frame_q == o, bias_ref[z, j], bias)
    for t in range(TOKENS):
        at = pl.ds(t, 64, stride=TOKENS)
        s = lax.dot_general(
            kt[at, :].astype(BF16), qt[at, :].astype(BF16), NT, preferred_element_type=F32
        ) * SCALE + bias
        top = jnp.max(s, axis=0, keepdims=True)
        e = jnp.exp(s - top)
        e_t[t] = e
        stat_t[0, t : t + 1, 0:64] = top
        stat_t[0, 24 + t : 25 + t, 0:64] = jnp.sum(e, axis=0, keepdims=True)
    send_ts("a")

    wait_y(1)
    unpack_first(spat_tile(1), spat_pair, qs, ks)

    def tile_at(n):
        j, b = lax.div(n, 3), lax.rem(n, 3)
        return (
            j,
            pl.ds(pl.multiple_of(j * ROWS, 8), ROWS),
            pl.ds(pl.multiple_of(j * ROWS + b * 256, 8), 256),
            pl.ds(pl.multiple_of(b * 256, 128), 256),
        )

    def scores(n):
        j, keys_at, rows_at, lanes_at = tile_at(n)
        s = lax.dot_general(
            ks[keys_at, :].astype(BF16), qs[rows_at, :].astype(BF16), NT,
            preferred_element_type=F32,
        ) * SCALE
        top = jnp.max(s, axis=0, keepdims=True)
        e = jnp.exp(s - top)
        e_s[j, :, lanes_at] = e
        stat_s[0, pl.ds(j, 1), lanes_at] = top
        stat_s[0, pl.ds(2 + j, 1), lanes_at] = jnp.sum(e, axis=0, keepdims=True)

    loop(0, 6, scores)
    send_st("a")

    forward(2, 1, 3)
    scale_t, other_t = scales(
        stat_t[0, 0:24, 0:64], stat_t[0, 24:48, 0:64], *got_s("a", 2)
    )
    wait_x(2)
    unpack_second(temp_tile(2, 1), temp_pair, gt)
    for t in range(TOKENS):
        at = pl.ds(t, 64, stride=TOKENS)
        rounded = (e_t[t] * scale_t[t : t + 1]).astype(BF16)
        p_t[t] = rounded
        vt[at, :] = jnp.dot(rounded, gt[at, :].astype(BF16), preferred_element_type=F32)

    def pack_values_t(n):
        own0, shared0, extra0 = value_tiles(load_rows(vt, 2 * n), 0)
        own1, shared1, extra1 = value_tiles(load_rows(vt, 2 * n + 1), 1)
        out = m["grad_tv"]
        out[n, 0] = own0.astype(BF16)
        out[n, 1] = (shared0 + shared1).astype(BF16)
        out[n, 2] = (extra0 + extra1).astype(BF16)
        out[n, 3] = own1.astype(BF16)

    loop(0, 16, pack_values_t)
    return_x("v")

    scale_own, scale_other = scales(stat_s[0, 0:2], stat_s[0, 2:4], *got_t("a", 2))
    scale_s[0:2] = scale_own
    scale_s[2:4] = scale_other

    def weights(n):
        j, _, _, lanes_at = tile_at(n)
        p_s[j, :, lanes_at] = (e_s[j, :, lanes_at] * scale_s[pl.ds(j, 1), lanes_at]).astype(BF16)

    loop(0, 6, weights)
    wait_y(2)
    unpack_second(spat_tile(2), spat_pair, gs)

    def value_grads(j):
        rows_at = pl.ds(pl.multiple_of(j * ROWS, 8), ROWS)
        vs[rows_at, :] = jnp.dot(
            p_s[j], gs[rows_at, :].astype(BF16), preferred_element_type=F32
        )

    loop(0, 2, value_grads)

    def pack_values_s(i):
        own, shared, extra = value_tiles(load_rows(vs, i), my_p)
        out = m["grad_sv"]
        out[i, 2 * my_p] = own.astype(BF16)
        out[i, 1 - my_p] = shared.astype(BF16)
        out[i, 2 - my_p] = extra.astype(BF16)

    loop(0, 32, pack_values_s)
    return_y("v")
    forward(3, 1, 2)
    go_home("v", 4, 1, 3)

    wait_x(3)
    unpack_third(temp_tile(3, 1), temp_tile(2, 1), temp_pair, vt)
    for t in range(TOKENS):
        at = pl.ds(t, 64, stride=TOKENS)
        d = lax.dot_general(
            vt[at, :].astype(BF16), gt[at, :].astype(BF16), NT, preferred_element_type=F32
        )
        d_t[t] = d
        stat_t[1, t : t + 1, 0:64] = jnp.sum(e_t[t] * d, axis=0, keepdims=True)
    send_ts("b")
    wait_y(3)
    unpack_third(spat_tile(3), spat_tile(2), spat_pair, vs)

    def dots(n):
        j, keys_at, rows_at, lanes_at = tile_at(n)
        d = lax.dot_general(
            vs[keys_at, :].astype(BF16), gs[rows_at, :].astype(BF16), NT,
            preferred_element_type=F32,
        )
        d_s[j, :, lanes_at] = d
        stat_s[1, pl.ds(j, 1), lanes_at] = jnp.sum(e_s[j, :, lanes_at] * d, axis=0, keepdims=True)

    loop(0, 6, dots)
    send_st("b")

    (moment_s,) = got_s("b", 1)
    delta_t = stat_t[1, 0:24, 0:64] * scale_t + moment_s * other_t
    for t in range(TOKENS):
        at = pl.ds(t, 64, stride=TOKENS)
        slope = (p_t[t].astype(F32) * (d_t[t] - delta_t[t : t + 1])).astype(BF16)
        k = kt[at, :].astype(BF16)
        q = qt[at, :].astype(BF16)
        kt[at, :] = jnp.dot(slope, q, preferred_element_type=F32) * SCALE
        across = slope.astype(F32).T.astype(BF16)
        qt[at, :] = jnp.dot(across, k, preferred_element_type=F32) * SCALE

    def pack_keys_t(n):
        main0, extra0 = key_tiles(load_rows(qt, 2 * n), load_rows(kt, 2 * n), 0)
        main1, extra1 = key_tiles(load_rows(qt, 2 * n + 1), load_rows(kt, 2 * n + 1), 1)
        out = m["grad_tk"]
        for r in range(3):
            out[n, r] = main0[r].astype(BF16)
            out[n, 4 + r] = main1[r].astype(BF16)
        out[n, 3] = (extra0 + extra1).astype(BF16)

    loop(0, 16, pack_keys_t)
    return_x("k")

    (moment_t,) = got_t("b", 1)
    scale_s[4:6] = stat_s[1, 0:2] * scale_s[0:2] + moment_t * scale_s[2:4]

    def slopes(n):
        j, _, _, lanes_at = tile_at(n)
        gap = d_s[j, :, lanes_at] - scale_s[pl.ds(4 + j, 1), lanes_at]
        sl_s[j, :, lanes_at] = (p_s[j, :, lanes_at].astype(F32) * gap).astype(BF16)

    loop(0, 6, slopes)

    def key_grads(j):
        rows_at = pl.ds(pl.multiple_of(j * ROWS, 8), ROWS)
        q = qs[rows_at, :].astype(BF16)
        k_turned = ks[rows_at, :].T.astype(BF16)
        ks[rows_at, :] = jnp.dot(sl_s[j], q, preferred_element_type=F32) * SCALE
        qs[rows_at, :] = jnp.dot(k_turned, sl_s[j], preferred_element_type=F32).T * SCALE

    loop(0, 2, key_grads)

    def pack_keys_s(i):
        main, extra = key_tiles(load_rows(qs, i), load_rows(ks, i), my_p)
        out = m["grad_sk"]
        for r in range(3):
            out[i, r + my_p] = main[r].astype(BF16)
        out[i, 3 - 3 * my_p] = extra.astype(BF16)

    loop(0, 32, pack_keys_s)
    return_y("k")
    go_home("k", 7, 3, 4)

    wait_home("v")
    restore_values(m["landedv"], dv_out)
    for c in (1, 2, 3):
        drain(c)
    for c in ("a", "b"):
        drain_stats(c)
    drain_back("v")
    wait_home("k")
    restore_keys(m["landedk"], dq_out, dk_out)
    drain_back("k")


def body(queries, keys, values, out_grad, time_bias):
    vmem = pl.BlockSpec(memory_space=pltpu.VMEM)
    shape = jax.ShapeDtypeStruct(queries.shape, BF16)
    shapes = scratch()

    def run(*refs):
        kernel(list(shapes), *refs)

    return pl.pallas_call(
        run,
        out_shape=(shape, shape, shape),
        in_specs=[vmem] * 4 + [pl.BlockSpec(memory_space=pltpu.SMEM)],
        out_specs=(vmem, vmem, vmem),
        scratch_shapes=list(shapes.values()),
        compiler_params=pltpu.CompilerParams(
            collective_id=0, has_side_effects=True, vmem_limit_bytes=56 * 2**20
        ),
    )(queries, keys, values, out_grad, time_bias)


def solution(mesh):
    spec = P("tm", "tok", None)
    return jax.shard_map(
        body, mesh=mesh, in_specs=(spec, spec, spec, spec, P()),
        out_specs=(spec, spec, spec), check_vma=False,
    )
```

time: 822 us -> 162 us (0.20)
  the two profiles are of different devices: /device:TPU:35 before, /device:TPU:1 now
where the time goes in v2:
time: 162 us
  Pallas kernels  158 us (98%)
  local copies, waits for them, and re-layouts  3.38 us (2%)
    pallas_call x1, Pallas kernels, body(): pl.pallas_call(run, out_shape=(shape, shape, shape), in_specs=[vmem] * 4...  158 us
    unnamed x7, local copies, waits for them, and re-layouts  3.38 us

profile of v2, /device:TPU:1, one launch (start us, length us, event | category | flops | bytes accessed | tf_op | source)
XLA Modules:
  0.0 161.7 jit_solution(9663537628460465987)
XLA Ops:
  0.6 157.6 %shard_map.76 = (bf16[4,24,1152]{2,1,0:T(8,128)(2,1)}, bf16[4,24,1152]{2,1,0:T(8,128)(2,1)}, bf16[4,24,1152]{2,1,0:T(8,128)(2,1)}) custom-call(bf16[4,24,1152]{2,1,0:T(8,128)(2,1)} %refs_0_.1, bf16[4,24,1152]{2,1,0:T(8,128)(2,1)} %refs_1_.1, bf16[4,24,1152]{2,1,0:T(8,128)(2,1)} %refs_2_.1, bf16[4,24,1152]{2,1,0:T(8,128)(2,1)} %refs_3_.1, f32[16,16]{1,0:T(8,128)} %refs_4_.1), custom_call_target="tpu_custom_call" | custom-call | tf_op jit(solution)/shard_map/pallas_call | solution.py:779
  158.3 0.0 copy-start.1
  158.3 1.7 %copy.11 = bf16[4,24,1152]{2,1,0:T(8,128)(2,1)} copy(bf16[4,24,1152]{2,1,0:T(8,128)(2,1)} %get-tuple-element.6) | data formatting | bytes 442368
  160.0 0.0 copy-done.1
  160.0 0.0 copy-start
  160.0 0.7 copy.12
  160.7 0.3 copy-done
  161.0 0.7 copy.13
Async XLA Ops:
  158.3 1.7 %copy-start.1 = (bf16[4,24,1152]{2,1,0:T(8,128)(2,1)S(1)}, bf16[4,24,1152]{2,1,0:T(8,128)(2,1)}, u32[]{:S(2)}) copy-start(bf16[4,24,1152]{2,1,0:T(8,128)(2,1)} %get-tuple-element.7) | copy-start | bytes 663556
  160.0 1.0 copy-start

commit v3 on v2

--- a/solution.py
+++ b/solution.py
@@ -94,87 +94,92 @@
         out_g[head, 2] = extra.astype(BF16)
 
 
-def store_rows(ref, i, value):
-    for j in range(2):
-        at = pl.ds(pl.multiple_of(j * ROWS + i * TOKENS, 8), TOKENS)
-        ref[at, :] = value[j * TOKENS : (j + 1) * TOKENS]
-
-
-def load_rows(ref, i):
-    return jnp.concatenate(
-        [
-            ref[pl.ds(pl.multiple_of(j * ROWS + i * TOKENS, 8), TOKENS), :]
-            for j in range(2)
-        ],
-        axis=0,
-    )
-
-
-def unpack_first(tile, pair_of, q_ref, k_ref):
+def open_first(plane, wide, source):
+    lane = lanes_of(16)
+    extra = plane[source, 3].astype(F32)
+    for p in range(2):
+        for r in range(3):
+            main = plane[source, 4 * p + r].astype(F32)
+            k = jnp.where(lane >= DIM, main, turn(extra, -48 * p - 16 * r))
+            wide[source, p, r] = jnp.where(lane < DIM, main, 0.0).astype(BF16)
+            wide[source, p, 3 + r] = turn(k, 56).astype(BF16)
+
+
+def open_second(plane, wide, source):
+    lane = lanes_of(16)
+    shared = plane[source, 1].astype(F32)
+    extra = plane[source, 2].astype(F32)
+    for p in range(2):
+        own = plane[source, 3 * p].astype(F32)
+        for r, main in enumerate((own, turn(own, 64), turn(shared, 64 * p))):
+            tail = jnp.where(lane < DIM, turn(extra, 64 - 48 * p - 16 * r), 0.0)
+            wide[source, p, r] = jnp.where(lane < 64, main, tail).astype(BF16)
+
+
+def open_third(plane, plane_g, wide, source):
+    lane = lanes_of(16)
+    shared = plane[source, 1].astype(F32)
+    extra = plane_g[source, 2].astype(F32)
+    for p in range(2):
+        own = plane[source, 2 * p].astype(F32)
+        for r, main in enumerate((turn(own, 8), turn(own, 72), turn(shared, 8 - 64 * p))):
+            head = turn(extra, -8 - 48 * p - 16 * r)
+            wide[source, p, r] = jnp.where(lane < 8, head, main).astype(BF16)
+
+
+def gather_rows(tiles, first, ref):
     def one(i, _):
-        lane = lanes_of(PAIR)
-        p = pair_of(i)
-        main = jnp.concatenate([tile(i, r + p).astype(F32) for r in range(3)], axis=0)
-        extra = tile(i, 3 - 3 * p).astype(F32)
-        extra = jnp.concatenate([turn(extra, -48 * p - 16 * r) for r in range(3)], axis=0)
-        store_rows(q_ref, i, jnp.where(lane < DIM, main, 0.0))
-        store_rows(k_ref, i, turn(jnp.where(lane >= DIM, main, extra), 56))
+        value = jnp.concatenate([tiles[i, first + r].astype(F32) for r in range(3)], axis=0)
+        for j in range(2):
+            at = pl.ds(pl.multiple_of(j * ROWS + i * TOKENS, 8), TOKENS)
+            ref[at, :] = value[j * TOKENS : (j + 1) * TOKENS]
         return 0
 
-    lax.fori_loop(0, GROUPS, one, 0)
-
-
-def unpack_second(tile, pair_of, g_ref):
+    lax.fori_loop(0, GROUPS, one, 0, unroll=8)
+
+
+def scatter_rows(ref, tiles, first):
     def one(i, _):
-        lane = lanes_of(PAIR)
-        p = pair_of(i)
-        own = tile(i, 2 * p).astype(F32)
-        shared = tile(i, 1 - p).astype(F32)
-        extra = tile(i, 2 - p).astype(F32)
-        main = jnp.concatenate([own, turn(own, 64), turn(shared, 64 * p)], axis=0)
-        tail = jnp.concatenate([turn(extra, 64 - 48 * p - 16 * r) for r in range(3)], axis=0)
-        store_rows(g_ref, i, jnp.where(lane < 64, main, jnp.where(lane < DIM, tail, 0.0)))
+        value = jnp.concatenate(
+            [
+                ref[pl.ds(pl.multiple_of(j * ROWS + i * TOKENS, 8), TOKENS), :]
+                for j in range(2)
+            ],
+            axis=0,
+        )
+        for r in range(3):
+            tiles[i, first + r] = group(value, r).astype(BF16)
         return 0
 
-    lax.fori_loop(0, GROUPS, one, 0)
-
-
-def unpack_third(tile, tile_g, pair_of, v_ref):
-    def one(i, _):
-        lane = lanes_of(PAIR)
-        p = pair_of(i)
-        own = tile(i, p).astype(F32)
-        shared = tile(i, 1 - p).astype(F32)
-        extra = tile_g(i, 2 - p).astype(F32)
-        main = jnp.concatenate([turn(own, 8), turn(own, 72), turn(shared, 8 - 64 * p)], axis=0)
-        head = jnp.concatenate([turn(extra, -8 - 48 * p - 16 * r) for r in range(3)], axis=0)
-        store_rows(v_ref, i, jnp.where(lane < 8, head, jnp.where(lane < DIM, main, 0.0)))
-        return 0
-
-    lax.fori_loop(0, GROUPS, one, 0)
-
-
-def value_tiles(dv, p):
-    lane16 = lanes_of(16)
-    half = lane16 < 64
-    own = jnp.where(half, group(dv, 0), turn(group(dv, 1), 64))
-    shared = turn(jnp.where(half, group(dv, 2), 0.0), 64 * p)
-    extra = jnp.zeros_like(own)
-    for r in reversed(range(3)):
-        inside = (lane16 >= 16 * r) & (lane16 < 16 * r + 8)
-        extra = jnp.where(inside, turn(group(dv, r), 16 * r - 64), extra)
-    return own, shared, turn(extra, 48 * p)
-
-
-def key_tiles(dq, dk, p):
-    lane, lane16 = lanes_of(PAIR), lanes_of(16)
-    dk = turn(dk, 72)
-    main = jnp.where(lane < DIM, dq, dk)
-    extra = jnp.zeros((16, 128), F32)
-    for r in range(3):
-        inside = (lane16 >= 16 * r) & (lane16 < 16 * r + 16)
-        extra = jnp.where(inside, turn(group(dk, r), 16 * r), extra)
-    return [group(main, r) for r in range(3)], turn(extra, 48 * p)
+    lax.fori_loop(0, GROUPS, one, 0, unroll=8)
+
+
+def close_values(dv, out, to):
+    lane = lanes_of(16)
+    half = lane < 64
+    for p in range(2):
+        out[to, 3 * p] = jnp.where(half, dv[p][0], turn(dv[p][1], 64)).astype(BF16)
+    out[to, 1] = jnp.where(half, dv[0][2], turn(dv[1][2], 64)).astype(BF16)
+    extra = None
+    for p in range(2):
+        for r in range(3):
+            low = 16 * (3 * p + r)
+            piece = turn(dv[p][r], low - 64)
+            extra = piece if extra is None else jnp.where(lane >= low, piece, extra)
+    out[to, 2] = extra.astype(BF16)
+
+
+def close_keys(dq, dk, out, to):
+    lane = lanes_of(16)
+    extra = None
+    for p in range(2):
+        for r in range(3):
+            low = 16 * (3 * p + r)
+            k = turn(dk[p][r], 72)
+            out[to, 4 * p + r] = jnp.where(lane < DIM, dq[p][r], k).astype(BF16)
+            piece = turn(k, low)
+            extra = piece if extra is None else jnp.where(lane >= low, piece, extra)
+    out[to, 3] = extra.astype(BF16)
 
 
 def spread_heads(parts, out, pair):
@@ -238,16 +243,17 @@
     square = (2, ROWS, ROWS)
     small = (TOKENS, 64, 64)
     shapes = {}
-    for n, (whole, part) in {1: (7, 4), 2: (4, 3), 3: (3, 2)}.items():
+    for n, (whole, part) in {1: (7, 6), 2: (4, 3), 3: (3, 3)}.items():
         shapes[f"send{n}"] = tiles(16, whole)
         shapes[f"plane{n}"] = tiles(16, whole)
-        shapes[f"temp{n}"] = tiles(16, whole)
+        shapes[f"wide{n}"] = pltpu.VMEM((16, 2, part, 16, 128), BF16)
+        shapes[f"temp{n}"] = tiles(32, part)
         shapes[f"spat{n}"] = tiles(32, part)
         for name, count in (("zs", 16), ("zr", 16), ("xs", 16), ("xr", 16), ("ys", 32), ("yr", 32)):
             shapes[f"{name}{n}"] = dma((count,))
-    for n, (whole, part) in {"v": (4, 3), "k": (7, 4)}.items():
-        shapes[f"grad_t{n}"] = tiles(16, whole)
-        shapes[f"back_t{n}"] = tiles(16, whole)
+    for n, (whole, part) in {"v": (4, 3), "k": (7, 6)}.items():
+        shapes[f"grad_t{n}"] = tiles(32, part)
+        shapes[f"back_t{n}"] = pltpu.VMEM((16, 2, part, 16, 128), BF16)
         shapes[f"final{n}"] = tiles(16, whole)
         shapes[f"landed{n}"] = tiles(16, whole)
         shapes[f"grad_s{n}"] = tiles(32, part)
@@ -350,23 +356,25 @@
     send_line(2)
     send_line(3)
 
-    def forward(c, shift, part):
-        plane, temp, spat = m[f"plane{c}"], m[f"temp{c}"], m[f"spat{c}"]
+    def forward(c, unpack):
+        plane, wide, temp, spat = m[f"plane{c}"], m[f"wide{c}"], m[f"temp{c}"], m[f"spat{c}"]
 
         def one(n):
             source = lax.rem(z + 16 - far_step(n), 16)
             hi, lo = lax.div(source, 8), lax.rem(source, 8)
             arrived(plane.at[source], m[f"zr{c}"].at[source])
+            unpack(source)
             to_x, to_core = lax.div(lo, 2), lax.rem(lo, 2)
             slot = 4 * x + 2 * hi + core
             start(
-                plane.at[source], temp.at[slot], m[f"xs{c}"].at[source], m[f"xr{c}"].at[slot],
+                wide.at[source], temp.at[pl.ds(pl.multiple_of(2 * slot, 2), 2)],
+                m[f"xs{c}"].at[source], m[f"xr{c}"].at[slot],
                 device(to_x, z, to_core, y), lo == spot,
             )
             for p in range(2):
                 to_y = 2 * hi + p
                 start(
-                    plane.at[source, pl.ds(shift * p, part)], spat.at[y * 8 + lo],
+                    wide.at[source, p], spat.at[y * 8 + lo],
                     m[f"ys{c}"].at[2 * source + p], m[f"yr{c}"].at[y * 8 + lo],
                     device(x, z, core, to_y), to_y == y,
                 )
@@ -374,22 +382,13 @@
         loop(1, 17, one)
 
     def wait_x(c):
-        loop(0, 16, lambda n: arrived(m[f"temp{c}"].at[n], m[f"xr{c}"].at[n]))
+        def one(n):
+            arrived(m[f"temp{c}"].at[pl.ds(pl.multiple_of(2 * n, 2), 2)], m[f"xr{c}"].at[n])
+
+        loop(0, 16, one)
 
     def wait_y(c):
         loop(0, 32, lambda n: arrived(m[f"spat{c}"].at[n], m[f"yr{c}"].at[n]))
-
-    def temp_tile(c, shift):
-        return lambda i, t: m[f"temp{c}"][lax.div(i, 2), t + shift * lax.rem(i, 2)]
-
-    def spat_tile(c):
-        return lambda i, t: m[f"spat{c}"][i, t]
-
-    def temp_pair(i):
-        return lax.rem(i, 2)
-
-    def spat_pair(i):
-        return my_p
 
     def send_ts(c):
         to_s, from_t = m["to_s" + c], m["from_t" + c]
@@ -487,8 +486,9 @@
             hi, there = lax.rem(n, 2), lax.rem(spot + lax.div(n, 2), 8)
             to_x, to_core = lax.div(there, 2), lax.rem(there, 2)
             source = hi * 8 + spot
+            block = pl.ds(pl.multiple_of(2 * (4 * to_x + 2 * hi + to_core), 2), 2)
             start(
-                grad.at[4 * to_x + 2 * hi + to_core], back.at[source],
+                grad.at[block], back.at[source],
                 m["bxs" + c].at[hi * 8 + there], m["bxr" + c].at[source],
                 device(to_x, z, to_core, y), there == spot,
             )
@@ -509,7 +509,7 @@
 
         loop(0, 32, one)
 
-    def go_home(c, whole, shift, part):
+    def go_home(c, close):
         back_s, back_t, final = m["back_s" + c], m["back_t" + c], m["final" + c]
 
         def one(n):
@@ -519,12 +519,18 @@
             for p in range(2):
                 slot = (2 * hi + p) * 8 + lo
                 arrived(back_s.at[slot], m["byr" + c].at[slot])
-            for t in range(whole):
-                total = back_t[to, t].astype(F32)
-                for p in range(2):
-                    if 0 <= t - shift * p < part:
-                        total = total + back_s[(2 * hi + p) * 8 + lo, t - shift * p].astype(F32)
-                final[to, t] = total.astype(BF16)
+
+            def total(first):
+                return [
+                    [
+                        back_t[to, p, first + r].astype(F32)
+                        + back_s[(2 * hi + p) * 8 + lo, first + r].astype(F32)
+                        for r in range(3)
+                    ]
+                    for p in range(2)
+                ]
+
+            close(total, final, to)
             start(
                 final.at[to], m["landed" + c].at[z], m["bzs" + c].at[to], m["bzr" + c].at[z],
                 device(x, to, core, y), to == z,
@@ -539,7 +545,7 @@
         def one(n):
             hi, lo = lax.div(n, 8), lax.rem(n, 8)
             sent(m[f"send{c}"].at[n], m[f"zs{c}"].at[n], n == z)
-            sent(m[f"plane{c}"].at[n], m[f"xs{c}"].at[n], lo == spot)
+            sent(m[f"wide{c}"].at[n], m[f"xs{c}"].at[n], lo == spot)
             for p in range(2):
                 sent(m[f"spat{c}"].at[n], m[f"ys{c}"].at[2 * n + p], 2 * hi + p == y)
 
@@ -548,7 +554,7 @@
     def drain_back(c):
         def one(n):
             sent(m["final" + c].at[n], m["bzs" + c].at[n], n == z)
-            sent(m["grad_t" + c].at[n], m["bxs" + c].at[n], lax.rem(n, 8) == spot)
+            sent(m["back_t" + c].at[n], m["bxs" + c].at[n], lax.rem(n, 8) == spot)
 
         loop(0, 16, one)
         loop(
@@ -572,9 +578,10 @@
     stat_s[...] = jnp.zeros_like(stat_s)
     stat_t[...] = jnp.zeros_like(stat_t)
 
-    forward(1, 3, 4)
+    forward(1, lambda source: open_first(m["plane1"], m["wide1"], source))
     wait_x(1)
-    unpack_first(temp_tile(1, 3), temp_pair, qt, kt)
+    gather_rows(m["temp1"], 0, qt)
+    gather_rows(m["temp1"], 3, kt)
     frame_k = lax.broadcasted_iota(jnp.int32, (64, 64), 0)
     frame_q = lax.broadcasted_iota(jnp.int32, (64, 64), 1)
     frame_k = 2 * lax.rem(frame_k, 32) + lax.div(frame_k, 32)
@@ -596,7 +603,8 @@
     send_ts("a")
 
     wait_y(1)
-    unpack_first(spat_tile(1), spat_pair, qs, ks)
+    gather_rows(m["spat1"], 0, qs)
+    gather_rows(m["spat1"], 3, ks)
 
     def tile_at(n):
         j, b = lax.div(n, 3), lax.rem(n, 3)
@@ -622,28 +630,19 @@
     loop(0, 6, scores)
     send_st("a")
 
-    forward(2, 1, 3)
+    forward(2, lambda source: open_second(m["plane2"], m["wide2"], source))
     scale_t, other_t = scales(
         stat_t[0, 0:24, 0:64], stat_t[0, 24:48, 0:64], *got_s("a", 2)
     )
     wait_x(2)
-    unpack_second(temp_tile(2, 1), temp_pair, gt)
+    gather_rows(m["temp2"], 0, gt)
     for t in range(TOKENS):
         at = pl.ds(t, 64, stride=TOKENS)
         rounded = (e_t[t] * scale_t[t : t + 1]).astype(BF16)
         p_t[t] = rounded
         vt[at, :] = jnp.dot(rounded, gt[at, :].astype(BF16), preferred_element_type=F32)
 
-    def pack_values_t(n):
-        own0, shared0, extra0 = value_tiles(load_rows(vt, 2 * n), 0)
-        own1, shared1, extra1 = value_tiles(load_rows(vt, 2 * n + 1), 1)
-        out = m["grad_tv"]
-        out[n, 0] = own0.astype(BF16)
-        out[n, 1] = (shared0 + shared1).astype(BF16)
-        out[n, 2] = (extra0 + extra1).astype(BF16)
-        out[n, 3] = own1.astype(BF16)
-
-    loop(0, 16, pack_values_t)
+    scatter_rows(vt, m["grad_tv"], 0)
     return_x("v")
 
     scale_own, scale_other = scales(stat_s[0, 0:2], stat_s[0, 2:4], *got_t("a", 2))
@@ -656,7 +655,7 @@
 
     loop(0, 6, weights)
     wait_y(2)
-    unpack_second(spat_tile(2), spat_pair, gs)
+    gather_rows(m["spat2"], 0, gs)
 
     def value_grads(j):
         rows_at = pl.ds(pl.multiple_of(j * ROWS, 8), ROWS)
@@ -666,20 +665,13 @@
 
     loop(0, 2, value_grads)
 
-    def pack_values_s(i):
-        own, shared, extra = value_tiles(load_rows(vs, i), my_p)
-        out = m["grad_sv"]
-        out[i, 2 * my_p] = own.astype(BF16)
-        out[i, 1 - my_p] = shared.astype(BF16)
-        out[i, 2 - my_p] = extra.astype(BF16)
-
-    loop(0, 32, pack_values_s)
+    scatter_rows(vs, m["grad_sv"], 0)
     return_y("v")
-    forward(3, 1, 2)
-    go_home("v", 4, 1, 3)
+    forward(3, lambda source: open_third(m["plane3"], m["plane2"], m["wide3"], source))
+    go_home("v", lambda total, out, to: close_values(total(0), out, to))
 
     wait_x(3)
-    unpack_third(temp_tile(3, 1), temp_tile(2, 1), temp_pair, vt)
+    gather_rows(m["temp3"], 0, vt)
     for t in range(TOKENS):
         at = pl.ds(t, 64, stride=TOKENS)
         d = lax.dot_general(
@@ -689,7 +681,7 @@
         stat_t[1, t : t + 1, 0:64] = jnp.sum(e_t[t] * d, axis=0, keepdims=True)
     send_ts("b")
     wait_y(3)
-    unpack_third(spat_tile(3), spat_tile(2), spat_pair, vs)
+    gather_rows(m["spat3"], 0, vs)
 
     def dots(n):
         j, keys_at, rows_at, lanes_at = tile_at(n)
@@ -714,16 +706,8 @@
         across = slope.astype(F32).T.astype(BF16)
         qt[at, :] = jnp.dot(across, k, preferred_element_type=F32) * SCALE
 
-    def pack_keys_t(n):
-        main0, extra0 = key_tiles(load_rows(qt, 2 * n), load_rows(kt, 2 * n), 0)
-        main1, extra1 = key_tiles(load_rows(qt, 2 * n + 1), load_rows(kt, 2 * n + 1), 1)
-        out = m["grad_tk"]
-        for r in range(3):
-            out[n, r] = main0[r].astype(BF16)
-            out[n, 4 + r] = main1[r].astype(BF16)
-        out[n, 3] = (extra0 + extra1).astype(BF16)
-
-    loop(0, 16, pack_keys_t)
+    scatter_rows(qt, m["grad_tk"], 0)
+    scatter_rows(kt, m["grad_tk"], 3)
     return_x("k")
 
     (moment_t,) = got_t("b", 1)
@@ -745,16 +729,10 @@
 
     loop(0, 2, key_grads)
 
-    def pack_keys_s(i):
-        main, extra = key_tiles(load_rows(qs, i), load_rows(ks, i), my_p)
-        out = m["grad_sk"]
-        for r in range(3):
-            out[i, r + my_p] = main[r].astype(BF16)
-        out[i, 3 - 3 * my_p] = extra.astype(BF16)
-
-    loop(0, 32, pack_keys_s)
+    scatter_rows(qs, m["grad_sk"], 0)
+    scatter_rows(ks, m["grad_sk"], 3)
     return_y("k")
-    go_home("k", 7, 3, 4)
+    go_home("k", lambda total, out, to: close_keys(total(0), total(3), out, to))
 
     wait_home("v")
     restore_values(m["landedv"], dv_out)

time: 162 us -> 131 us (0.81)
  Pallas kernels: 158 us -> 127 us
    pallas_call x1, Pallas kernels: 158 us -> 127 us  [body(): pl.pallas_call(run, out_shape=(shape, shape, shape), in_specs=[vmem] * 4...]
where the time goes in v3:
time: 131 us
  Pallas kernels  127 us (97%)
  local copies, waits for them, and re-layouts  3.38 us (3%)
    pallas_call x1, Pallas kernels, body(): pl.pallas_call(run, out_shape=(shape, shape, shape), in_specs=[vmem] * 4...  127 us
    unnamed x7, local copies, waits for them, and re-layouts  3.38 us

profile of v3, /device:TPU:1, one launch (start us, length us, event | category | flops | bytes accessed | tf_op | source)
XLA Modules:
  0.0 131.2 jit_solution(6269267931118725972)
XLA Ops:
  0.6 127.1 %shard_map.76 = (bf16[4,24,1152]{2,1,0:T(8,128)(2,1)}, bf16[4,24,1152]{2,1,0:T(8,128)(2,1)}, bf16[4,24,1152]{2,1,0:T(8,128)(2,1)}) custom-call(bf16[4,24,1152]{2,1,0:T(8,128)(2,1)} %refs_0_.1, bf16[4,24,1152]{2,1,0:T(8,128)(2,1)} %refs_1_.1, bf16[4,24,1152]{2,1,0:T(8,128)(2,1)} %refs_2_.1, bf16[4,24,1152]{2,1,0:T(8,128)(2,1)} %refs_3_.1, f32[16,16]{1,0:T(8,128)} %refs_4_.1), custom_call_target="tpu_custom_call" | custom-call | tf_op jit(solution)/shard_map/pallas_call | solution.py:757
  127.8 0.0 copy-start.1
  127.8 1.7 %copy.11 = bf16[4,24,1152]{2,1,0:T(8,128)(2,1)} copy(bf16[4,24,1152]{2,1,0:T(8,128)(2,1)} %get-tuple-element.6) | data formatting | bytes 442368
  129.5 0.0 copy-done.1
  129.5 0.0 copy-start
  129.5 0.7 copy.12
  130.1 0.3 copy-done
  130.5 0.7 copy.13
Async XLA Ops:
  127.8 1.7 %copy-start.1 = (bf16[4,24,1152]{2,1,0:T(8,128)(2,1)S(1)}, bf16[4,24,1152]{2,1,0:T(8,128)(2,1)}, u32[]{:S(2)}) copy-start(bf16[4,24,1152]{2,1,0:T(8,128)(2,1)} %get-tuple-element.7) | copy-start | bytes 663556
  129.5 1.0 copy-start

commit v4 on v3

--- a/solution.py
+++ b/solution.py
@@ -249,8 +249,9 @@
         shapes[f"wide{n}"] = pltpu.VMEM((16, 2, part, 16, 128), BF16)
         shapes[f"temp{n}"] = tiles(32, part)
         shapes[f"spat{n}"] = tiles(32, part)
-        for name, count in (("zs", 16), ("zr", 16), ("xs", 16), ("xr", 16), ("ys", 32), ("yr", 32)):
-            shapes[f"{name}{n}"] = dma((count,))
+        shapes[f"zr{n}"] = dma((16,))
+        for name in ("zs", "xs", "xr", "ys", "yr"):
+            shapes[f"{name}{n}"] = dma
     for n, (whole, part) in {"v": (4, 3), "k": (7, 6)}.items():
         shapes[f"grad_t{n}"] = tiles(32, part)
         shapes[f"back_t{n}"] = pltpu.VMEM((16, 2, part, 16, 128), BF16)
@@ -258,10 +259,9 @@
         shapes[f"landed{n}"] = tiles(16, whole)
         shapes[f"grad_s{n}"] = tiles(32, part)
         shapes[f"back_s{n}"] = tiles(32, part)
-        for name, count in (
-            ("bxs", 16), ("bxr", 16), ("bys", 32), ("byr", 32), ("bzs", 16), ("bzr", 16),
-        ):
-            shapes[f"{name}{n}"] = dma((count,))
+        shapes[f"br{n}"] = dma((16,))
+        for name in ("bxs", "bys", "bzs", "bzr"):
+            shapes[f"{name}{n}"] = dma
     for name in ("qs", "ks", "vs", "gs", "qt", "kt", "vt", "gt"):
         shapes[name] = wide
     shapes.update(
@@ -275,7 +275,7 @@
         for name in ("to_s", "to_t", "from_s", "from_t"):
             shapes[name + n] = pltpu.VMEM((256, 128), F32)
         for name in ("tss", "tsr", "sts", "str"):
-            shapes[name + n] = dma((32,))
+            shapes[name + n] = dma
     return shapes
 
 
@@ -309,11 +309,6 @@
     def arrived(ref, sem):
         pltpu.make_async_copy(ref, ref, sem).wait()
 
-    def sent(ref, sem, here):
-        @pl.when(jnp.logical_not(here))
-        def _():
-            pltpu.make_async_copy(ref, ref, sem).wait()
-
     def loop(low, high, step):
         def one(n, _):
             step(n)
@@ -343,7 +338,7 @@
         def one(n):
             to = lax.rem(z + far_step(n), 16)
             start(
-                send.at[to], plane.at[z], m[f"zs{c}"].at[to], m[f"zr{c}"].at[z],
+                send.at[to], plane.at[z], m[f"zs{c}"], m[f"zr{c}"].at[z],
                 device(x, to, core, y), to == z,
             )
 
@@ -368,27 +363,24 @@
             slot = 4 * x + 2 * hi + core
             start(
                 wide.at[source], temp.at[pl.ds(pl.multiple_of(2 * slot, 2), 2)],
-                m[f"xs{c}"].at[source], m[f"xr{c}"].at[slot],
+                m[f"xs{c}"], m[f"xr{c}"],
                 device(to_x, z, to_core, y), lo == spot,
             )
             for p in range(2):
                 to_y = 2 * hi + p
                 start(
                     wide.at[source, p], spat.at[y * 8 + lo],
-                    m[f"ys{c}"].at[2 * source + p], m[f"yr{c}"].at[y * 8 + lo],
+                    m[f"ys{c}"], m[f"yr{c}"],
                     device(x, z, core, to_y), to_y == y,
                 )
 
         loop(1, 17, one)
 
     def wait_x(c):
-        def one(n):
-            arrived(m[f"temp{c}"].at[pl.ds(pl.multiple_of(2 * n, 2), 2)], m[f"xr{c}"].at[n])
-
-        loop(0, 16, one)
+        arrived(m[f"temp{c}"], m[f"xr{c}"])
 
     def wait_y(c):
-        loop(0, 32, lambda n: arrived(m[f"spat{c}"].at[n], m[f"yr{c}"].at[n]))
+        arrived(m[f"spat{c}"], m[f"yr{c}"])
 
     def send_ts(c):
         to_s, from_t = m["to_s" + c], m["from_t" + c]
@@ -403,7 +395,7 @@
             start(
                 to_s.at[pl.ds(pl.multiple_of(r * 8, 8), 8)],
                 from_t.at[pl.ds(pl.multiple_of(my_group * 8, 8), 8)],
-                m["tss" + c].at[r], m["tsr" + c].at[my_group],
+                m["tss" + c], m["tsr" + c],
                 device(lax.div(r, 8), z, lax.rem(lax.div(r, 2), 2), to_y), r == my_pair,
             )
 
@@ -427,7 +419,7 @@
             start(
                 to_t.at[pl.ds(pl.multiple_of(i * 8, 8), 8)],
                 from_s.at[pl.ds(pl.multiple_of(my_pair * 8, 8), 8)],
-                m["sts" + c].at[i], m["str" + c].at[my_pair],
+                m["sts" + c], m["str" + c],
                 device(lax.div(lo, 2), z, lax.rem(lo, 2), lax.div(i, 8)), i == my_group,
             )
 
@@ -435,11 +427,7 @@
 
     def got_s(c, count):
         from_s = m["from_s" + c]
-
-        def one(n):
-            arrived(from_s.at[pl.ds(pl.multiple_of(n * 8, 8), 8)], m["str" + c].at[n])
-
-        loop(0, 32, one)
+        arrived(from_s, m["str" + c])
         return [
             jnp.concatenate(
                 [from_s[pl.ds(2 * n + j, 32, stride=8), :] for j in range(2)], axis=0
@@ -449,11 +437,7 @@
 
     def got_t(c, count):
         from_t = m["from_t" + c]
-
-        def one(n):
-            arrived(from_t.at[pl.ds(pl.multiple_of(n * 8, 8), 8)], m["tsr" + c].at[n])
-
-        loop(0, 32, one)
+        arrived(from_t, m["tsr" + c])
         lane = lax.broadcasted_iota(jnp.int32, (64, ROWS), 1)
         row = lax.broadcasted_iota(jnp.int32, (64, ROWS), 0)
         own = lax.div(lane, TOKENS) == lax.rem(row, 32)
@@ -489,7 +473,7 @@
             block = pl.ds(pl.multiple_of(2 * (4 * to_x + 2 * hi + to_core), 2), 2)
             start(
                 grad.at[block], back.at[source],
-                m["bxs" + c].at[hi * 8 + there], m["bxr" + c].at[source],
+                m["bxs" + c], m["br" + c].at[source],
                 device(to_x, z, to_core, y), there == spot,
             )
 
@@ -503,7 +487,7 @@
             to_y = lax.rem(y + lax.rem(n, 4), 4)
             start(
                 grad.at[to_y * 8 + lo], back.at[y * 8 + lo],
-                m["bys" + c].at[to_y * 8 + lo], m["byr" + c].at[y * 8 + lo],
+                m["bys" + c], m["br" + c].at[8 * lax.div(y, 2) + lo],
                 device(x, z, core, to_y), to_y == y,
             )
 
@@ -515,10 +499,7 @@
         def one(n):
             to = lax.rem(z + far_step(n), 16)
             hi, lo = lax.div(to, 8), lax.rem(to, 8)
-            arrived(back_t.at[to], m["bxr" + c].at[to])
-            for p in range(2):
-                slot = (2 * hi + p) * 8 + lo
-                arrived(back_s.at[slot], m["byr" + c].at[slot])
+            arrived(back_s.at[0:4], m["br" + c].at[to])
 
             def total(first):
                 return [
@@ -532,43 +513,28 @@
 
             close(total, final, to)
             start(
-                final.at[to], m["landed" + c].at[z], m["bzs" + c].at[to], m["bzr" + c].at[z],
+                final.at[to], m["landed" + c].at[z], m["bzs" + c], m["bzr" + c],
                 device(x, to, core, y), to == z,
             )
 
         loop(1, 17, one)
 
     def wait_home(c):
-        loop(0, 16, lambda n: arrived(m["landed" + c].at[n], m["bzr" + c].at[n]))
+        arrived(m["landed" + c], m["bzr" + c])
 
     def drain(c):
-        def one(n):
-            hi, lo = lax.div(n, 8), lax.rem(n, 8)
-            sent(m[f"send{c}"].at[n], m[f"zs{c}"].at[n], n == z)
-            sent(m[f"wide{c}"].at[n], m[f"xs{c}"].at[n], lo == spot)
-            for p in range(2):
-                sent(m[f"spat{c}"].at[n], m[f"ys{c}"].at[2 * n + p], 2 * hi + p == y)
-
-        loop(0, 16, one)
+        arrived(m[f"send{c}"].at[0:15], m[f"zs{c}"])
+        arrived(m[f"wide{c}"].at[0:14], m[f"xs{c}"])
+        arrived(m[f"spat{c}"].at[0:24], m[f"ys{c}"])
 
     def drain_back(c):
-        def one(n):
-            sent(m["final" + c].at[n], m["bzs" + c].at[n], n == z)
-            sent(m["back_t" + c].at[n], m["bxs" + c].at[n], lax.rem(n, 8) == spot)
-
-        loop(0, 16, one)
-        loop(
-            0, 32,
-            lambda n: sent(m["grad_s" + c].at[n], m["bys" + c].at[n], lax.div(n, 8) == y),
-        )
+        arrived(m["final" + c].at[0:15], m["bzs" + c])
+        arrived(m["back_t" + c].at[0:14], m["bxs" + c])
+        arrived(m["grad_s" + c].at[0:24], m["bys" + c])
 
     def drain_stats(c):
-        def one(n):
-            at = pl.ds(pl.multiple_of(n * 8, 8), 8)
-            sent(m["to_s" + c].at[at], m["tss" + c].at[n], n == my_pair)
-            sent(m["to_t" + c].at[at], m["sts" + c].at[n], n == my_group)
-
-        loop(0, 32, one)
+        arrived(m["to_s" + c].at[0:248], m["tss" + c])
+        arrived(m["to_t" + c].at[0:248], m["sts" + c])
 
     qs, ks, vs, gs = m["qs"], m["ks"], m["vs"], m["gs"]
     qt, kt, vt, gt = m["qt"], m["kt"], m["vt"], m["gt"]

time: 131 us -> 123 us (0.939)
  Pallas kernels: 127 us -> 119 us
    pallas_call x1, Pallas kernels: 127 us -> 119 us  [body(): pl.pallas_call(run, out_shape=(shape, shape, shape), in_specs=[vmem] * 4...]
where the time goes in v4:
time: 123 us
  Pallas kernels  119 us (97%)
  local copies, waits for them, and re-layouts  3.38 us (3%)
    pallas_call x1, Pallas kernels, body(): pl.pallas_call(run, out_shape=(shape, shape, shape), in_specs=[vmem] * 4...  119 us
    unnamed x7, local copies, waits for them, and re-layouts  3.38 us

profile of v4, /device:TPU:1, one launch (start us, length us, event | category | flops | bytes accessed | tf_op | source)
XLA Modules:
  0.0 122.9 jit_solution(2884328095295734410)
XLA Ops:
  0.6 118.9 %shard_map.76 = (bf16[4,24,1152]{2,1,0:T(8,128)(2,1)}, bf16[4,24,1152]{2,1,0:T(8,128)(2,1)}, bf16[4,24,1152]{2,1,0:T(8,128)(2,1)}) custom-call(bf16[4,24,1152]{2,1,0:T(8,128)(2,1)} %refs_0_.1, bf16[4,24,1152]{2,1,0:T(8,128)(2,1)} %refs_1_.1, bf16[4,24,1152]{2,1,0:T(8,128)(2,1)} %refs_2_.1, bf16[4,24,1152]{2,1,0:T(8,128)(2,1)} %refs_3_.1, f32[16,16]{1,0:T(8,128)} %refs_4_.1), custom_call_target="tpu_custom_call" | custom-call | tf_op jit(solution)/shard_map/pallas_call | solution.py:723
  119.5 0.0 copy-start.1
  119.5 1.7 %copy.11 = bf16[4,24,1152]{2,1,0:T(8,128)(2,1)} copy(bf16[4,24,1152]{2,1,0:T(8,128)(2,1)} %get-tuple-element.6) | data formatting | bytes 442368
  121.2 0.0 copy-done.1
  121.2 0.0 copy-start
  121.2 0.7 copy.12
  121.9 0.3 copy-done
  122.2 0.7 copy.13
Async XLA Ops:
  119.5 1.7 %copy-start.1 = (bf16[4,24,1152]{2,1,0:T(8,128)(2,1)S(1)}, bf16[4,24,1152]{2,1,0:T(8,128)(2,1)}, u32[]{:S(2)}) copy-start(bf16[4,24,1152]{2,1,0:T(8,128)(2,1)} %get-tuple-element.7) | copy-start | bytes 663556
  121.2 1.0 copy-start

commit v5 on v4

--- a/solution.py
+++ b/solution.py
@@ -169,17 +169,38 @@
     out[to, 2] = extra.astype(BF16)
 
 
-def close_keys(dq, dk, out, to):
+def scatter_keys(q_ref, k_ref, tiles):
+    def one(i, _):
+        lane, lane16 = lanes_of(PAIR), lanes_of(16)
+        dq, dk = (
+            jnp.concatenate(
+                [
+                    ref[pl.ds(pl.multiple_of(j * ROWS + i * TOKENS, 8), TOKENS), :]
+                    for j in range(2)
+                ],
+                axis=0,
+            )
+            for ref in (q_ref, k_ref)
+        )
+        dk = turn(dk, 72)
+        main = jnp.where(lane < DIM, dq, dk)
+        extra = group(dk, 0)
+        for r in range(1, 3):
+            extra = jnp.where(lane16 >= 16 * r, turn(group(dk, r), 16 * r), extra)
+        for r in range(3):
+            tiles[i, r] = group(main, r).astype(BF16)
+        tiles[i, 3] = extra.astype(BF16)
+        return 0
+
+    lax.fori_loop(0, GROUPS, one, 0, unroll=8)
+
+
+def close_keys(main, extra, out, to):
     lane = lanes_of(16)
-    extra = None
     for p in range(2):
         for r in range(3):
-            low = 16 * (3 * p + r)
-            k = turn(dk[p][r], 72)
-            out[to, 4 * p + r] = jnp.where(lane < DIM, dq[p][r], k).astype(BF16)
-            piece = turn(k, low)
-            extra = piece if extra is None else jnp.where(lane >= low, piece, extra)
-    out[to, 3] = extra.astype(BF16)
+            out[to, 4 * p + r] = main[p][r].astype(BF16)
+    out[to, 3] = jnp.where(lane < 48, extra[0][0], turn(extra[1][0], 48)).astype(BF16)
 
 
 def spread_heads(parts, out, pair):
@@ -190,7 +211,8 @@
             low, high = head * DIM - 128 * t, head * DIM + DIM - 128 * t
             if high <= 0 or low >= 128:
                 continue
-            whole = parts[head] if whole is None else jnp.where(lane < high, parts[head], whole)
+            part = parts[head][...]
+            whole = part if whole is None else jnp.where(lane < high, part, whole)
         for j in range(2):
             out[2 * pair + j, :, 128 * t : 128 * t + 128] = whole[
                 TOKENS * j : TOKENS * j + TOKENS
@@ -213,20 +235,24 @@
         spread_heads(parts, dv_out, pair)
 
 
-def restore_keys(landed, dq_out, dk_out):
+def place_keys(landed, q_parts, k_parts, head):
+    lane = lanes_of(PAIR)
+    extra_tile = landed[head, 3].astype(F32)
     for pair in range(2):
-        lane = lanes_of(PAIR)
-        q_parts, k_parts = [], []
-        for head in range(HEADS):
-            main = jnp.concatenate(
-                [landed[head, 4 * pair + r].astype(F32) for r in range(3)], axis=0
-            )
-            extra = landed[head, 3].astype(F32)
-            extra = jnp.concatenate([turn(extra, -48 * pair - 16 * r) for r in range(3)], axis=0)
-            q_parts.append(turn(main, head * DIM))
-            k_parts.append(turn(jnp.where(lane >= DIM, main, extra), head * DIM - DIM))
-        spread_heads(q_parts, dq_out, pair)
-        spread_heads(k_parts, dk_out, pair)
+        main = jnp.concatenate(
+            [landed[head, 4 * pair + r].astype(F32) for r in range(3)], axis=0
+        )
+        extra = jnp.concatenate(
+            [turn(extra_tile, -48 * pair - 16 * r) for r in range(3)], axis=0
+        )
+        q_parts[head, pair] = turn(main, head * DIM)
+        k_parts[head, pair] = turn(jnp.where(lane >= DIM, main, extra), head * DIM - DIM)
+
+
+def restore_keys(q_parts, k_parts, dq_out, dk_out):
+    for pair in range(2):
+        for parts, out in ((q_parts, dq_out), (k_parts, dk_out)):
+            spread_heads([parts.at[head, pair] for head in range(HEADS)], out, pair)
 
 
 def far_step(n):
@@ -252,7 +278,7 @@
         shapes[f"zr{n}"] = dma((16,))
         for name in ("zs", "xs", "xr", "ys", "yr"):
             shapes[f"{name}{n}"] = dma
-    for n, (whole, part) in {"v": (4, 3), "k": (7, 6)}.items():
+    for n, (whole, part) in {"v": (4, 3), "k": (7, 4)}.items():
         shapes[f"grad_t{n}"] = tiles(32, part)
         shapes[f"back_t{n}"] = pltpu.VMEM((16, 2, part, 16, 128), BF16)
         shapes[f"final{n}"] = tiles(16, whole)
@@ -260,8 +286,15 @@
         shapes[f"grad_s{n}"] = tiles(32, part)
         shapes[f"back_s{n}"] = tiles(32, part)
         shapes[f"br{n}"] = dma((16,))
-        for name in ("bxs", "bys", "bzs", "bzr"):
+        for name in ("bxs", "bys", "bzs"):
             shapes[f"{name}{n}"] = dma
+    shapes["bzrv"] = dma((1,))
+    shapes["bzrk"] = dma((16,))
+    for name in ("q_in", "k_in", "v_in", "g_in"):
+        shapes[name] = pltpu.VMEM((4, TOKENS, WIDTH), BF16)
+    shapes["load"] = dma((4,))
+    for name in ("q_parts", "k_parts"):
+        shapes[name] = pltpu.VMEM((HEADS, 2, PAIR, 128), F32)
     for name in ("qs", "ks", "vs", "gs", "qt", "kt", "vt", "gt"):
         shapes[name] = wide
     shapes.update(
@@ -279,8 +312,9 @@
     return shapes
 
 
-def kernel(names, q_in, k_in, v_in, g_in, bias_ref, dq_out, dk_out, dv_out, *refs):
+def kernel(names, q_hbm, k_hbm, v_hbm, g_hbm, bias_ref, dq_out, dk_out, dv_out, *refs):
     m = dict(zip(names, refs, strict=True))
+    q_in, k_in, v_in, g_in = (m[name] for name in ("q_in", "k_in", "v_in", "g_in"))
     tm = lax.axis_index("tm")
     tok = lax.axis_index("tok")
     x, zhi, core = lax.div(tm, 4), lax.rem(lax.div(tm, 2), 2), lax.rem(tm, 2)
@@ -331,6 +365,16 @@
         hail(device(lax.div(there, 2), z, lax.rem(there, 2), lax.div(other, 8)))
 
     loop(1, 32, hail_plane)
+    loads = [
+        pltpu.make_async_copy(source, target, m["load"].at[n])
+        for n, (source, target) in enumerate(
+            ((q_hbm, q_in), (k_hbm, k_in), (g_hbm, g_in), (v_hbm, v_in))
+        )
+    ]
+    for load in loads:
+        load.start()
+    loads[0].wait()
+    loads[1].wait()
 
     def send_line(c):
         send, plane = m[f"send{c}"], m[f"plane{c}"]
@@ -347,6 +391,8 @@
     pack_first(q_in, k_in, m["send1"])
     pl.semaphore_wait(barrier, 46)
     send_line(1)
+    loads[2].wait()
+    loads[3].wait()
     pack_second(g_in, v_in, m["send2"], m["send3"])
     send_line(2)
     send_line(3)
@@ -501,26 +547,28 @@
             hi, lo = lax.div(to, 8), lax.rem(to, 8)
             arrived(back_s.at[0:4], m["br" + c].at[to])
 
-            def total(first):
+            def total(first, count):
                 return [
                     [
                         back_t[to, p, first + r].astype(F32)
                         + back_s[(2 * hi + p) * 8 + lo, first + r].astype(F32)
-                        for r in range(3)
+                        for r in range(count)
                     ]
                     for p in range(2)
                 ]
 
             close(total, final, to)
             start(
-                final.at[to], m["landed" + c].at[z], m["bzs" + c], m["bzr" + c],
+                final.at[to], m["landed" + c].at[z], m["bzs" + c], m["bzr" + c].at[z if c == "k" else 0],
                 device(x, to, core, y), to == z,
             )
 
         loop(1, 17, one)
 
-    def wait_home(c):
-        arrived(m["landed" + c], m["bzr" + c])
+    def home_keys(n):
+        head = lax.rem(z + 16 - far_step(n), 16)
+        arrived(m["landedk"].at[head], m["bzrk"].at[head])
+        place_keys(m["landedk"], m["q_parts"], m["k_parts"], head)
 
     def drain(c):
         arrived(m[f"send{c}"].at[0:15], m[f"zs{c}"])
@@ -601,6 +649,7 @@
         stat_t[0, 0:24, 0:64], stat_t[0, 24:48, 0:64], *got_s("a", 2)
     )
     wait_x(2)
+    forward(3, lambda source: open_third(m["plane3"], m["plane2"], m["wide3"], source))
     gather_rows(m["temp2"], 0, gt)
     for t in range(TOKENS):
         at = pl.ds(t, 64, stride=TOKENS)
@@ -633,8 +682,6 @@
 
     scatter_rows(vs, m["grad_sv"], 0)
     return_y("v")
-    forward(3, lambda source: open_third(m["plane3"], m["plane2"], m["wide3"], source))
-    go_home("v", lambda total, out, to: close_values(total(0), out, to))
 
     wait_x(3)
     gather_rows(m["temp3"], 0, vt)
@@ -660,6 +707,7 @@
 
     loop(0, 6, dots)
     send_st("b")
+    go_home("v", lambda total, out, to: close_values(total(0, 3), out, to))
 
     (moment_s,) = got_s("b", 1)
     delta_t = stat_t[1, 0:24, 0:64] * scale_t + moment_s * other_t
@@ -672,8 +720,7 @@
         across = slope.astype(F32).T.astype(BF16)
         qt[at, :] = jnp.dot(across, k, preferred_element_type=F32) * SCALE
 
-    scatter_rows(qt, m["grad_tk"], 0)
-    scatter_rows(kt, m["grad_tk"], 3)
+    scatter_keys(qt, kt, m["grad_tk"])
     return_x("k")
 
     (moment_t,) = got_t("b", 1)
@@ -695,20 +742,19 @@
 
     loop(0, 2, key_grads)
 
-    scatter_rows(qs, m["grad_sk"], 0)
-    scatter_rows(ks, m["grad_sk"], 3)
+    scatter_keys(qs, ks, m["grad_sk"])
     return_y("k")
-    go_home("k", lambda total, out, to: close_keys(total(0), total(3), out, to))
-
-    wait_home("v")
+    go_home("k", lambda total, out, to: close_keys(total(0, 3), total(3, 1), out, to))
+
+    arrived(m["landedv"], m["bzrv"].at[0])
     restore_values(m["landedv"], dv_out)
     for c in (1, 2, 3):
         drain(c)
     for c in ("a", "b"):
         drain_stats(c)
     drain_back("v")
-    wait_home("k")
-    restore_keys(m["landedk"], dq_out, dk_out)
+    loop(1, 17, home_keys)
+    restore_keys(m["q_parts"], m["k_parts"], dq_out, dk_out)
     drain_back("k")
 
 
@@ -722,8 +768,8 @@
 
     return pl.pallas_call(
         run,
-        out_shape=(shape, shape, shape),
-        in_specs=[vmem] * 4 + [pl.BlockSpec(memory_space=pltpu.SMEM)],
+        out_shape=tuple(pltpu.VMEM(queries.shape, BF16) for _ in range(3)),
+        in_specs=[pl.BlockSpec(memory_space=pl.ANY)] * 4 + [pl.BlockSpec(memory_space=pltpu.SMEM)],
         out_specs=(vmem, vmem, vmem),
         scratch_shapes=list(shapes.values()),
         compiler_params=pltpu.CompilerParams(

time: 123 us -> 115 us (0.935)
  Pallas kernels: 119 us -> 112 us
  local copies, waits for them, and re-layouts: 3.38 us -> 2.06 us
    pallas_call x1, Pallas kernels: 119 us -> 112 us  [body(): pl.pallas_call(run, out_shape=tuple((pltpu.VMEM(queries.shape, BF16) for...]
    unnamed x7 -> x3, local copies, waits for them, and re-layouts: 3.38 us -> 2.06 us
where the time goes in v5:
time: 115 us; the launch traced here: 114 us
  Pallas kernels  112 us (97%)
  local copies, waits for them, and re-layouts  2.06 us (2%)
    pallas_call x1, Pallas kernels, body(): pl.pallas_call(run, out_shape=tuple((pltpu.VMEM(queries.shape, BF16) for...  112 us

profile of v5, /device:TPU:1, one launch (start us, length us, event | category | flops | bytes accessed | tf_op | source)
XLA Modules:
  0.0 114.4 jit_solution(17838981387833228549)
XLA Ops:
  0.6 111.7 %shard_map.76 = (bf16[4,24,1152]{2,1,0:T(8,128)(2,1)S(1)}, bf16[4,24,1152]{2,1,0:T(8,128)(2,1)S(1)}, bf16[4,24,1152]{2,1,0:T(8,128)(2,1)S(1)}) custom-call(bf16[4,24,1152]{2,1,0:T(8,128)(2,1)} %refs_0_.1, bf16[4,24,1152]{2,1,0:T(8,128)(2,1)} %refs_1_.1, bf16[4,24,1152]{2,1,0:T(8,128)(2,1)} %refs_2_.1, bf16[4,24,1152]{2,1,0:T(8,128)(2,1)} %refs_3_.1, ...), custom_call_target="tpu_custom_call" | custom-call | tf_op jit(solution)/shard_map/pallas_call | solution.py:769
  112.4 0.7 copy.11
  113.1 0.7 copy.12
  113.7 0.7 copy.13

commit v6 on v5

--- a/solution.py
+++ b/solution.py
@@ -303,6 +303,8 @@
         e_t=pltpu.VMEM(small, F32), d_t=pltpu.VMEM(small, F32), p_t=pltpu.VMEM(small, BF16),
         stat_s=pltpu.VMEM((2, 8, ROWS), F32), scale_s=pltpu.VMEM((8, ROWS), F32),
         stat_t=pltpu.VMEM((2, 128, 128), F32),
+        own_wide=pltpu.VMEM((256, ROWS), F32), own=pltpu.VMEM((64, ROWS), F32),
+        pick=pltpu.VMEM((ROWS, 128), F32), repeat=pltpu.VMEM((2, 128, ROWS), F32),
     )
     for n in ("a", "b"):
         for name in ("to_s", "to_t", "from_s", "from_t"):
@@ -388,7 +390,25 @@
 
         loop(1, 17, one)
 
+    def make_masks():
+        def place(rows, lanes):
+            return (
+                lax.broadcasted_iota(jnp.int32, (rows, lanes), 0),
+                lax.broadcasted_iota(jnp.int32, (rows, lanes), 1),
+            )
+
+        row, lane = place(256, ROWS)
+        m["own_wide"][...] = (lax.div(lane, TOKENS) == lax.div(row, 8)).astype(F32)
+        row, lane = place(64, ROWS)
+        m["own"][...] = (lax.div(lane, TOKENS) == lax.rem(row, 32)).astype(F32)
+        row, lane = place(ROWS, 128)
+        m["pick"][...] = (lax.rem(row, TOKENS) == lane).astype(F32)
+        row, lane = place(128, ROWS)
+        for n in range(2):
+            m["repeat"][n] = (lax.rem(lane, TOKENS) == row - TOKENS * n).astype(F32)
+
     pack_first(q_in, k_in, m["send1"])
+    make_masks()
     pl.semaphore_wait(barrier, 46)
     send_line(1)
     loads[2].wait()
@@ -397,14 +417,11 @@
     send_line(2)
     send_line(3)
 
-    def forward(c, unpack):
+    def forward(c, unpack, step, low=0, high=16):
         plane, wide, temp, spat = m[f"plane{c}"], m[f"wide{c}"], m[f"temp{c}"], m[f"spat{c}"]
 
-        def one(n):
-            source = lax.rem(z + 16 - far_step(n), 16)
+        def pass_on(source):
             hi, lo = lax.div(source, 8), lax.rem(source, 8)
-            arrived(plane.at[source], m[f"zr{c}"].at[source])
-            unpack(source)
             to_x, to_core = lax.div(lo, 2), lax.rem(lo, 2)
             slot = 4 * x + 2 * hi + core
             start(
@@ -420,7 +437,16 @@
                     device(x, z, core, to_y), to_y == y,
                 )
 
-        loop(1, 17, one)
+        def one(n):
+            sources = [lax.rem(z + 16 - far_step(step * n + k + 1), 16) for k in range(step)]
+            for source in sources:
+                arrived(plane.at[source], m[f"zr{c}"].at[source])
+            for source in sources:
+                unpack(source)
+            for source in sources:
+                pass_on(source)
+
+        loop(low // step, high // step, one)
 
     def wait_x(c):
         arrived(m[f"temp{c}"], m[f"xr{c}"])
@@ -435,41 +461,41 @@
         for j in range(2):
             to_s[pl.ds(j, 32, stride=8), :] = turned[32 * j : 32 * j + 32]
 
+        landing = from_t.at[pl.ds(pl.multiple_of(my_group * 8, 8), 8)]
+
         def one(n):
             r = lax.rem(my_pair + n, 32)
             to_y = 2 * lax.rem(lax.div(r, 4), 2) + lax.rem(r, 2)
-            start(
-                to_s.at[pl.ds(pl.multiple_of(r * 8, 8), 8)],
-                from_t.at[pl.ds(pl.multiple_of(my_group * 8, 8), 8)],
-                m["tss" + c], m["tsr" + c],
-                device(lax.div(r, 8), z, lax.rem(lax.div(r, 2), 2), to_y), r == my_pair,
-            )
-
-        loop(0, 32, one)
+            remote(
+                to_s.at[pl.ds(pl.multiple_of(r * 8, 8), 8)], landing, m["tss" + c], m["tsr" + c],
+                device(lax.div(r, 8), z, lax.rem(lax.div(r, 2), 2), to_y),
+            ).start()
+
+        loop(1, 32, one)
+        here = to_s.at[pl.ds(pl.multiple_of(my_pair * 8, 8), 8)]
+        pltpu.make_async_copy(here, landing, m["tsr" + c]).start()
 
     def send_st(c):
         to_t, from_s = m["to_t" + c], m["from_s" + c]
         stat = m["stat_s"][0 if c == "a" else 1]
-        row = lax.broadcasted_iota(jnp.int32, (256, ROWS), 0)
-        lane = lax.broadcasted_iota(jnp.int32, (256, ROWS), 1)
-        own = lax.div(lane, TOKENS) == lax.div(row, 8)
-        spread = jnp.where(own, jnp.concatenate([stat] * 32, axis=0), 0.0)
-        row = lax.broadcasted_iota(jnp.int32, (ROWS, 128), 0)
-        lane = lax.broadcasted_iota(jnp.int32, (ROWS, 128), 1)
-        pick = (lax.rem(row, TOKENS) == lane).astype(F32)
-        to_t[...] = jnp.dot(spread, pick, precision=HIGHEST, preferred_element_type=F32)
+        spread = m["own_wide"][...] * jnp.concatenate([stat] * 32, axis=0)
+        to_t[...] = jnp.dot(
+            spread, m["pick"][...], precision=HIGHEST, preferred_element_type=F32
+        )
+
+        landing = from_s.at[pl.ds(pl.multiple_of(my_pair * 8, 8), 8)]
 
         def one(n):
             i = lax.rem(my_group + n, 32)
             lo = lax.rem(i, 8)
-            start(
-                to_t.at[pl.ds(pl.multiple_of(i * 8, 8), 8)],
-                from_s.at[pl.ds(pl.multiple_of(my_pair * 8, 8), 8)],
-                m["sts" + c], m["str" + c],
-                device(lax.div(lo, 2), z, lax.rem(lo, 2), lax.div(i, 8)), i == my_group,
-            )
-
-        loop(0, 32, one)
+            remote(
+                to_t.at[pl.ds(pl.multiple_of(i * 8, 8), 8)], landing, m["sts" + c], m["str" + c],
+                device(lax.div(lo, 2), z, lax.rem(lo, 2), lax.div(i, 8)),
+            ).start()
+
+        loop(1, 32, one)
+        here = to_t.at[pl.ds(pl.multiple_of(my_group * 8, 8), 8)]
+        pltpu.make_async_copy(here, landing, m["str" + c]).start()
 
     def got_s(c, count):
         from_s = m["from_s" + c]
@@ -484,17 +510,11 @@
     def got_t(c, count):
         from_t = m["from_t" + c]
         arrived(from_t, m["tsr" + c])
-        lane = lax.broadcasted_iota(jnp.int32, (64, ROWS), 1)
-        row = lax.broadcasted_iota(jnp.int32, (64, ROWS), 0)
-        own = lax.div(lane, TOKENS) == lax.rem(row, 32)
         got = jnp.concatenate([from_t[pl.ds(j, 32, stride=8), :] for j in range(2)], axis=0)
-        lane = lax.broadcasted_iota(jnp.int32, (128, ROWS), 1)
-        row = lax.broadcasted_iota(jnp.int32, (128, ROWS), 0)
         found = []
         for n in range(count):
-            repeat = (lax.rem(lane, TOKENS) == row - TOKENS * n).astype(F32)
-            wide = jnp.dot(got, repeat, precision=HIGHEST, preferred_element_type=F32)
-            wide = jnp.where(own, wide, 0.0)
+            wide = jnp.dot(got, m["repeat"][n], precision=HIGHEST, preferred_element_type=F32)
+            wide = wide * m["own"][...]
             found.append(
                 jnp.concatenate(
                     [jnp.sum(wide[32 * j : 32 * j + 32], axis=0, keepdims=True) for j in range(2)],
@@ -592,7 +612,7 @@
     stat_s[...] = jnp.zeros_like(stat_s)
     stat_t[...] = jnp.zeros_like(stat_t)
 
-    forward(1, lambda source: open_first(m["plane1"], m["wide1"], source))
+    forward(1, lambda source: open_first(m["plane1"], m["wide1"], source), 1)
     wait_x(1)
     gather_rows(m["temp1"], 0, qt)
     gather_rows(m["temp1"], 3, kt)
@@ -616,6 +636,7 @@
         stat_t[0, 24 + t : 25 + t, 0:64] = jnp.sum(e, axis=0, keepdims=True)
     send_ts("a")
 
+    forward(2, lambda source: open_second(m["plane2"], m["wide2"], source), 2, 0, 8)
     wait_y(1)
     gather_rows(m["spat1"], 0, qs)
     gather_rows(m["spat1"], 3, ks)
@@ -644,12 +665,13 @@
     loop(0, 6, scores)
     send_st("a")
 
-    forward(2, lambda source: open_second(m["plane2"], m["wide2"], source))
+    forward(2, lambda source: open_second(m["plane2"], m["wide2"], source), 2, 8, 16)
+    forward(3, lambda source: open_third(m["plane3"], m["plane2"], m["wide3"], source), 2, 0, 8)
     scale_t, other_t = scales(
         stat_t[0, 0:24, 0:64], stat_t[0, 24:48, 0:64], *got_s("a", 2)
     )
     wait_x(2)
-    forward(3, lambda source: open_third(m["plane3"], m["plane2"], m["wide3"], source))
+    forward(3, lambda source: open_third(m["plane3"], m["plane2"], m["wide3"], source), 2, 8, 16)
     gather_rows(m["temp2"], 0, gt)
     for t in range(TOKENS):
         at = pl.ds(t, 64, stride=TOKENS)

time: 115 us -> 112 us (0.974)
  Pallas kernels: 112 us -> 109 us
    pallas_call x1, Pallas kernels: 112 us -> 109 us  [body(): pl.pallas_call(run, out_shape=tuple((pltpu.VMEM(queries.shape, BF16) for...]
where the time goes in v6:
time: 112 us
  Pallas kernels  109 us (97%)
  local copies, waits for them, and re-layouts  2.06 us (2%)
    pallas_call x1, Pallas kernels, body(): pl.pallas_call(run, out_shape=tuple((pltpu.VMEM(queries.shape, BF16) for...  109 us

profile of v6, /device:TPU:1, one launch (start us, length us, event | category | flops | bytes accessed | tf_op | source)
XLA Modules:
  0.0 112.2 jit_solution(7279605631619275855)
XLA Ops:
  0.6 109.5 %shard_map.76 = (bf16[4,24,1152]{2,1,0:T(8,128)(2,1)S(1)}, bf16[4,24,1152]{2,1,0:T(8,128)(2,1)S(1)}, bf16[4,24,1152]{2,1,0:T(8,128)(2,1)S(1)}) custom-call(bf16[4,24,1152]{2,1,0:T(8,128)(2,1)} %refs_0_.1, bf16[4,24,1152]{2,1,0:T(8,128)(2,1)} %refs_1_.1, bf16[4,24,1152]{2,1,0:T(8,128)(2,1)} %refs_2_.1, bf16[4,24,1152]{2,1,0:T(8,128)(2,1)} %refs_3_.1, ...), custom_call_target="tpu_custom_call" | custom-call | tf_op jit(solution)/shard_map/pallas_call | solution.py:791
  110.1 0.7 copy.11
  110.8 0.7 copy.12
  111.5 0.7 copy.13
